TPU v7x, 32 devices: a whole 2x2x4 slice. The times are simulated.
32 devices in a mesh: rows: 8 (over z, x), feat: 4 (over y, core).
Axes of the slice: x: 2, y: 2, z: 4, core: 2. Of those that a mesh axis runs over, the one named last changes fastest.
Arguments:
- binned: int32 [16384, 256], P('rows', 'feat'), may hold values from 0 to 255
- node_index: int32 [16384, 1], P('rows'), may hold values from 0 to 7; in each aligned block of 2048 rows (0 to 2047, 2048 to 4095, ...) at most 512 rows name the same one
- treatment: float32 [16384], P('rows'), may hold values from -6 to 6
- outcome: float32 [16384], P('rows'), may hold values from -6 to 6
- unit_weight: float32 [16384], P('rows'), may hold values from 0.1 to 2
- root_feature: int32 [8], replicated, may hold values from 0 to 255
- root_cutoff: int32 [8], replicated, may hold values from 64 to 191
- child_feature: int32 [16], replicated, may hold values from 0 to 255
- child_cutoff: int32 [16], replicated, may hold values from 64 to 191
Outputs:
- node_moments: float32 [8, 3, 256, 256], P('rows', None, 'feat')
- child_moments: float32 [16, 3, 256, 256], P('rows', None, 'feat')
- leaf_moments: float32 [32, 3, 256, 256], P('rows', None, 'feat')
Inputs may be any that keep to these rules, and one draw needn't show every extreme that they name: `node_index`: among the rows of one device no node is named by more than 512 rows, a bound that some block reaches.
All inputs are finite; a program needn't handle non-finite values.
Results may differ from a plain program's by a relative error of at most 0.0022.
Values may be sent and summed in bfloat16 or wider, within the bound.
A program may use at most 64 MiB of HBM per device.

v0:
```python
import jax
import jax.numpy as jnp
from jax import lax
from jax.sharding import PartitionSpec as P

BINS = 256


def histogram(weighted, features):
    feat_count, unit_count = features.shape
    blocks = features.reshape(feat_count // 4, 4, unit_count)
    levels = jnp.arange(BINS).astype(features.dtype)

    def one_block(carry, block):
        table = (block[:, :, None] == levels).astype(jnp.bfloat16)
        part = jnp.einsum("sc,fsb->cfb", weighted, table, preferred_element_type=jnp.float32)
        return (carry, part)

    unused, parts = lax.scan(one_block, 0, blocks)
    return jnp.moveaxis(parts, 0, 1).reshape(weighted.shape[1], feat_count, BINS)


def weigh(groups, group_count, moments):
    chosen = groups[:, None] == jnp.arange(group_count)
    spread = jnp.where(chosen[:, :, None], moments[:, None, :], jnp.zeros((), jnp.bfloat16))
    return spread.reshape(moments.shape[0], group_count * 3)


def on_device(
    binned,
    node_index,
    treatment,
    outcome,
    unit_weight,
    root_feature,
    root_cutoff,
    child_feature,
    child_cutoff,
):
    rows_here, feat_here = binned.shape
    node_count = root_feature.shape[0]
    owners = lax.axis_size("rows")
    per_owner = node_count // owners
    capacity = 2 * rows_here // node_count
    tree_node = node_index[:, 0]
    moments = jnp.stack(
        [unit_weight, unit_weight * treatment * treatment, unit_weight * treatment * outcome], 1
    ).astype(jnp.bfloat16)
    feature_major = binned.T
    first_child = 2 * tree_node
    wanted = jnp.stack(
        [root_feature[tree_node], child_feature[first_child], child_feature[first_child + 1]], 0
    )
    wanted = wanted - lax.axis_index("feat") * feat_here
    local_index = jnp.arange(feat_here)
    picked = jnp.sum(jnp.where(wanted[:, :, None] == local_index, binned[None, :, :], 0), axis=2)
    split_values = lax.psum(picked.astype(jnp.float32), "feat").astype(jnp.int32)
    right_root = (split_values[0] > root_cutoff[tree_node]).astype(jnp.int32)
    right_child = jnp.where(
        right_root == 1,
        split_values[2] > child_cutoff[first_child + 1],
        split_values[1] > child_cutoff[first_child],
    ).astype(jnp.int32)
    leaf_code = 2 * right_root + right_child
    all_weighted = weigh(tree_node, node_count, moments)
    all_terms = histogram(all_weighted, feature_major).reshape(node_count, 3, feat_here, BINS)
    node_moments = lax.psum_scatter(all_terms, "rows", scatter_dimension=0, tiled=True)
    node_onehot = (tree_node[:, None] == jnp.arange(node_count)).astype(jnp.int32)
    rank_in_node = jnp.sum(jnp.cumsum(node_onehot, 0) * node_onehot, 1) - 1
    slot_index = tree_node * capacity + rank_in_node
    feat_buffer = (
        jnp.zeros((feat_here, node_count * capacity), jnp.bfloat16)
        .at[:, slot_index]
        .set(feature_major.astype(jnp.bfloat16))
    )
    carried = jnp.concatenate([moments.T, leaf_code[None, :].astype(jnp.bfloat16)], 0)
    moment_buffer = (
        jnp.zeros((4, node_count * capacity), jnp.bfloat16).at[:, slot_index].set(carried)
    )
    feat_buffer = feat_buffer.reshape(feat_here, owners, per_owner * capacity)
    moment_buffer = moment_buffer.reshape(4, owners, per_owner * capacity)
    got_feat, got_moment = (
        lax.all_to_all(feat_buffer, "rows", split_axis=1, concat_axis=1, tiled=True),
        lax.all_to_all(moment_buffer, "rows", split_axis=1, concat_axis=1, tiled=True),
    )
    slots = owners * per_owner * capacity
    got_feat = got_feat.reshape(feat_here, slots)
    got_moment = got_moment.reshape(4, slots)
    owned_node = jnp.arange(slots) % (per_owner * capacity) // capacity
    got_leaf = got_moment[3].astype(jnp.int32)
    got_values = got_moment[:3].T
    leaf_weighted = weigh(4 * owned_node + got_leaf, 4 * per_owner, got_values)
    leaf_moments = histogram(leaf_weighted, got_feat).reshape(4 * per_owner, 3, feat_here, BINS)
    child_moments = leaf_moments.reshape(2 * per_owner, 2, 3, feat_here, BINS).sum(1)
    return (node_moments, child_moments, leaf_moments)


def solution(mesh):
    in_specs = (
        P("rows", "feat"),
        P("rows", None),
        P("rows"),
        P("rows"),
        P("rows"),
        P(),
        P(),
        P(),
        P(),
    )
    out_specs = (
        P("rows", None, "feat", None),
        P("rows", None, "feat", None),
        P("rows", None, "feat", None),
    )
    return jax.shard_map(
        on_device, mesh=mesh, in_specs=in_specs, out_specs=out_specs, check_vma=False
    )
```

profile of v0, /device:TPU:0, one launch (start us, length us, event | category | flops | bytes accessed | tf_op | source)
XLA Modules:
  0.0 230.3 jit_solution(13967984133397886732)
XLA Ops:
  10.0 36.6 %while.22 = (s32[]{:T(128)}, f32[16,24,4,256]{3,1,2,0:T(8,128)S(1)}, s32[16,4,2048]{2,1,0:T(4,128)S(1)}, bf16[2048,3]{0,1:T(4,128)(2,1)S(1)}, pred[2048,8]{0,1:T(8,128)(4,1)S(1)}, /*index=5*/s32[]{:T(128)}) while((s32[]{:T(128)}, f32[16,24,4,256]{3,1,2,0:T(8,128)S(1)}, s32[16,4,2048]{2,1,0:T(4,128)S(1)}, ...), condition=%wide.region_1.2_spmd.clone, body=%wide.region_0.1_spmd.clone.sunk | while | flops 102809600 | bytes 618581 | solution.py:19
  51.0 8.9 %compare_select_fusion.5 = (s32[2048,1]{0,1:T(1,128)S(1)}, s32[2048,1]{0,1:T(1,128)S(1)}, s32[2048,1]{0,1:T(1,128)S(1)}, s32[2048,1]{0,1:T(1,128)S(1)}) fusion(s32[]{:T(128)} %bitcast.59, s32[]{:T(128)} %bitcast.60, s32[]{:T(128)} %bitcast.61, s32[]{:T(128)} %bitcast.62, s32[]{:T(128)} %bitcast.63, s32[]{:T(128)} %bitcast.65, s32[]{:T(128)} %bitcast.64, ...), kind=kLoop, calls=%fused_computation.69 | loop fusion | flops 65536 | bytes 41016 | tf_op jit(solution)/shard_map/gather | solution.py:61
  60.3 8.8 %compare_select_fusion.4 = (s32[2048,1]{0,1:T(1,128)S(1)}, s32[2048,1]{0,1:T(1,128)S(1)}) fusion(s32[2048,1]{0,1:T(1,128)S(1)} %get-tuple-element.128, s32[]{:T(128)} %bitcast.29, s32[]{:T(128)} %bitcast.30, s32[]{:T(128)} %bitcast.31, s32[]{:T(128)} %bitcast.32, s32[]{:T(128)} %bitcast.33, s32[]{:T(128)} %bitcast.35, s32[]{:T(128)} %bitcast.34, ...), kind=kLoop, calls=%fused_computation.68 | loop fusion | flops 49152 | bytes 32824 | tf_op jit(solution)/shard_map/gather | solution.py:52
  73.5 8.7 %compare_select_fusion.29 = (s32[2048,1]{0,1:T(1,128)S(1)}, s32[2048,1]{0,1:T(1,128)S(1)}, s32[2048,1]{0,1:T(1,128)S(1)}) fusion(s32[]{:T(128)} %bitcast.41, s32[]{:T(128)} %bitcast.42, s32[]{:T(128)} %bitcast.43, s32[]{:T(128)} %bitcast.44, s32[]{:T(128)} %bitcast.45, s32[]{:T(128)} %bitcast.47, s32[]{:T(128)} %bitcast.46, s32[2048,1]{0,1:T(1,128)S(1)} %copy-done.1, ...), kind=kLoop, calls=%fused_computation.93 | loop fusion | flops 53248 | bytes 41016 | tf_op jit(solution)/shard_map/gather | solution.py:58
  83.5 5.7 %select_select_fusion.2 = s32[2048]{0:T(1024)S(1)} fusion(pred[2048]{0:T(1024)(128)(4,1)S(1)} %get-tuple-element.97, pred[2048]{0:T(1024)(128)(4,1)S(1)} %get-tuple-element.96, pred[2048]{0:T(1024)(128)(4,1)S(1)} %get-tuple-element.95, pred[2048]{0:T(1024)(128)(4,1)S(1)} %get-tuple-element.94, pred[2048]{0:T(1024)(128)(4,1)S(1)} %get-tuple-element.93, ...), kind=kLoop, calls=%fused_computation.120 | loop fusion | flops 18432 | bytes 34852 | tf_op jit(solution)/shard_map/gather | solution.py:52
  89.2 5.7 %select_select_fusion.3 = s32[2048]{0:T(1024)S(1)} fusion(pred[2048]{0:T(1024)(128)(4,1)S(1)} %get-tuple-element.189, pred[2048]{0:T(1024)(128)(4,1)S(1)} %get-tuple-element.190, pred[2048]{0:T(1024)(128)(4,1)S(1)} %get-tuple-element.191, pred[2048]{0:T(1024)(128)(4,1)S(1)} %get-tuple-element.192, pred[2048]{0:T(1024)(128)(4,1)S(1)} %get-tuple-element.193, ...), kind=kLoop, calls=%fused_computation.121 | loop fusion | flops 18432 | bytes 34852 | tf_op jit(solution)/shard_map/gather | solution.py:52
  95.2 13.3 %psum.7 = f32[3,2048]{1,0:T(4,128)S(1)} all-reduce(f32[3,2048]{1,0:T(4,128)S(1)} %convert_element_type.50), channel_id=1, replica_groups=mesh['rows'=8,'feat'=4] {'feat'}, use_global_device_ids=true, to_apply=%region_8.9 | all-reduce | flops 6144 | bytes 49152 | tf_op jit(solution)/shard_map/psum | solution.py:57
  108.5 5.7 %select_select_fusion = s32[2048]{0:T(1024)S(1)} fusion(pred[2048]{0:T(1024)(128)(4,1)S(1)} %get-tuple-element.189, pred[2048]{0:T(1024)(128)(4,1)S(1)} %get-tuple-element.190, pred[2048]{0:T(1024)(128)(4,1)S(1)} %get-tuple-element.191, pred[2048]{0:T(1024)(128)(4,1)S(1)} %get-tuple-element.192, pred[2048]{0:T(1024)(128)(4,1)S(1)} %get-tuple-element.193, ...), kind=kLoop, calls=%fused_computation.118 | loop fusion | flops 18432 | bytes 34852 | tf_op jit(solution)/shard_map/gather | solution.py:62
  114.2 5.7 %select_select_fusion.1 = s32[2048]{0:T(1024)S(1)} fusion(pred[2048]{0:T(1024)(128)(4,1)S(1)} %get-tuple-element.97, pred[2048]{0:T(1024)(128)(4,1)S(1)} %get-tuple-element.96, pred[2048]{0:T(1024)(128)(4,1)S(1)} %get-tuple-element.95, pred[2048]{0:T(1024)(128)(4,1)S(1)} %get-tuple-element.94, pred[2048]{0:T(1024)(128)(4,1)S(1)} %get-tuple-element.93, ...), kind=kLoop, calls=%fused_computation.119 | loop fusion | flops 18432 | bytes 34852 | tf_op jit(solution)/shard_map/gather | solution.py:61
  120.3 6.1 %scatter_custom_fusion.1 = bf16[4,4096]{0,1:T(8,128)(2,1)S(1)} fusion(s32[2048]{0:T(1024)S(1)} %bitcast.154, bf16[2048,4]{1,0:T(8,128)(2,1)S(1)} %copy.48, bf16[]{:T(256)} %constant.69.clone.1), kind=kCustom, calls=%fused_computation.24 | custom fusion | bytes 32770 | tf_op jit(solution)/shard_map/scatter | solution.py:78
  127.4 5.8 %all-to-all-start.1 = ((bf16[4,8,512]{2,0,1:T(4,128)(2,1)}), bf16[4,8,512]{2,0,1:T(4,128)(2,1)S(1)}, u32[]{:S(2)}, u32[]{:S(2)}) async-start(bf16[4,8,512]{2,0,1:T(4,128)(2,1)} %copy.49), calls=%async_computation.2 | async-start | bytes 65536 | tf_op jit(solution)/shard_map/all_to_all | solution.py:84
  133.5 6.1 %scatter_custom_fusion = bf16[64,4096]{0,1:T(8,128)(2,1)S(1)} fusion(s32[2048]{0:T(1024)S(1)} %bitcast.155, bf16[2048,64]{1,0:T(8,128)(2,1)S(1)} %copy.45, bf16[]{:T(256)} %constant.69.clone.1), kind=kCustom, calls=%fused_computation.26 | custom fusion | bytes 524290 | tf_op jit(solution)/shard_map/scatter | solution.py:74
  140.7 6.0 %all-to-all-start = ((bf16[64,8,512]{2,0,1:T(8,128)(2,1)}), bf16[64,8,512]{2,0,1:T(8,128)(2,1)S(1)}, u32[]{:S(2)}, u32[]{:S(2)}) async-start(bf16[64,8,512]{2,0,1:T(8,128)(2,1)} %copy.46), calls=%async_computation.1 | async-start | bytes 1048576 | tf_op jit(solution)/shard_map/all_to_all | solution.py:83
  146.8 12.5 %all-to-all-done = bf16[64,8,512]{2,0,1:T(8,128)(2,1)S(1)} async-done(((bf16[64,8,512]{2,0,1:T(8,128)(2,1)}), bf16[64,8,512]{2,0,1:T(8,128)(2,1)S(1)}, u32[]{:S(2)}, u32[]{:S(2)}) %all-to-all-start) | async-done | bytes 524320 | tf_op jit(solution)/shard_map/all_to_all | solution.py:83
  160.0 60.7 %while.23 = (s32[]{:T(128)}, f32[16,12,4,256]{3,1,2,0:T(8,128)S(1)}, bf16[16,4,4096]{2,1,0:T(4,128)(2,1)S(1)}, bf16[4096,3]{0,1:T(4,128)(2,1)S(1)}, pred[4096,4]{0,1:T(4,128)(4,1)S(1)}, /*index=5*/s32[]{:T(128)}) while((s32[]{:T(128)}, f32[16,12,4,256]{3,1,2,0:T(8,128)S(1)}, bf16[16,4,4096]{2,1,0:T(4,128)(2,1)S(1)}, ...), condition=%wide.region_11.12_spmd.clone, body=%wide.region_10.11_spmd.clone.sunk | while | flops 104907008 | bytes 631893 | solution.py:19
  160.2 3.5 %fusion.53 = f32[16,12,4,256]{3,1,2,0:T(8,128)S(1)} fusion(f32[16,12,4,256]{3,1,2,0:T(8,128)S(1)} %get-tuple-element.287, s32[]{:T(128)S(6)} %copy.64, bf16[4096,12,1]{0,1,2:T(8,128)(2,1)S(1)} %reshape.526, bf16[256]{0:T(256)(128)(2,1)S(1)} %iota_convert_fusion.2, bf16[4,4096]{1,0:T(4,128)(2,1)S(1)} %dynamic-slice_bitcast_fusion.5), kind=kOutput, calls=%fused_computation.18.clone.1 | convolution fusion | flops 104857600 | bytes 229892 | tf_op jit(solution)/shard_map/while/body/eval_jaxpr/sc,fsb->cfb/dot_general | solution.py:16
  164.0 3.5 %fusion.53 = f32[16,12,4,256]{3,1,2,0:T(8,128)S(1)} fusion(f32[16,12,4,256]{3,1,2,0:T(8,128)S(1)} %get-tuple-element.287, s32[]{:T(128)S(6)} %copy.64, bf16[4096,12,1]{0,1,2:T(8,128)(2,1)S(1)} %reshape.526, bf16[256]{0:T(256)(128)(2,1)S(1)} %iota_convert_fusion.2, bf16[4,4096]{1,0:T(4,128)(2,1)S(1)} %dynamic-slice_bitcast_fusion.5), kind=kOutput, calls=%fused_computation.18.clone.1 | convolution fusion | flops 104857600 | bytes 229892 | tf_op jit(solution)/shard_map/while/body/eval_jaxpr/sc,fsb->cfb/dot_general | solution.py:16
  171.6 3.5 %fusion.53 = f32[16,12,4,256]{3,1,2,0:T(8,128)S(1)} fusion(f32[16,12,4,256]{3,1,2,0:T(8,128)S(1)} %get-tuple-element.287, s32[]{:T(128)S(6)} %copy.64, bf16[4096,12,1]{0,1,2:T(8,128)(2,1)S(1)} %reshape.526, bf16[256]{0:T(256)(128)(2,1)S(1)} %iota_convert_fusion.2, bf16[4,4096]{1,0:T(4,128)(2,1)S(1)} %dynamic-slice_bitcast_fusion.5), kind=kOutput, calls=%fused_computation.18.clone.1 | convolution fusion | flops 104857600 | bytes 229892 | tf_op jit(solution)/shard_map/while/body/eval_jaxpr/sc,fsb->cfb/dot_general | solution.py:16
  175.4 3.5 %fusion.53 = f32[16,12,4,256]{3,1,2,0:T(8,128)S(1)} fusion(f32[16,12,4,256]{3,1,2,0:T(8,128)S(1)} %get-tuple-element.287, s32[]{:T(128)S(6)} %copy.64, bf16[4096,12,1]{0,1,2:T(8,128)(2,1)S(1)} %reshape.526, bf16[256]{0:T(256)(128)(2,1)S(1)} %iota_convert_fusion.2, bf16[4,4096]{1,0:T(4,128)(2,1)S(1)} %dynamic-slice_bitcast_fusion.5), kind=kOutput, calls=%fused_computation.18.clone.1 | convolution fusion | flops 104857600 | bytes 229892 | tf_op jit(solution)/shard_map/while/body/eval_jaxpr/sc,fsb->cfb/dot_general | solution.py:16
  179.2 3.5 %fusion.53 = f32[16,12,4,256]{3,1,2,0:T(8,128)S(1)} fusion(f32[16,12,4,256]{3,1,2,0:T(8,128)S(1)} %get-tuple-element.287, s32[]{:T(128)S(6)} %copy.64, bf16[4096,12,1]{0,1,2:T(8,128)(2,1)S(1)} %reshape.526, bf16[256]{0:T(256)(128)(2,1)S(1)} %iota_convert_fusion.2, bf16[4,4096]{1,0:T(4,128)(2,1)S(1)} %dynamic-slice_bitcast_fusion.5), kind=kOutput, calls=%fused_computation.18.clone.1 | convolution fusion | flops 104857600 | bytes 229892 | tf_op jit(solution)/shard_map/while/body/eval_jaxpr/sc,fsb->cfb/dot_general | solution.py:16
  183.0 3.5 %fusion.53 = f32[16,12,4,256]{3,1,2,0:T(8,128)S(1)} fusion(f32[16,12,4,256]{3,1,2,0:T(8,128)S(1)} %get-tuple-element.287, s32[]{:T(128)S(6)} %copy.64, bf16[4096,12,1]{0,1,2:T(8,128)(2,1)S(1)} %reshape.526, bf16[256]{0:T(256)(128)(2,1)S(1)} %iota_convert_fusion.2, bf16[4,4096]{1,0:T(4,128)(2,1)S(1)} %dynamic-slice_bitcast_fusion.5), kind=kOutput, calls=%fused_computation.18.clone.1 | convolution fusion | flops 104857600 | bytes 229892 | tf_op jit(solution)/shard_map/while/body/eval_jaxpr/sc,fsb->cfb/dot_general | solution.py:16
  186.8 3.5 %fusion.53 = f32[16,12,4,256]{3,1,2,0:T(8,128)S(1)} fusion(f32[16,12,4,256]{3,1,2,0:T(8,128)S(1)} %get-tuple-element.287, s32[]{:T(128)S(6)} %copy.64, bf16[4096,12,1]{0,1,2:T(8,128)(2,1)S(1)} %reshape.526, bf16[256]{0:T(256)(128)(2,1)S(1)} %iota_convert_fusion.2, bf16[4,4096]{1,0:T(4,128)(2,1)S(1)} %dynamic-slice_bitcast_fusion.5), kind=kOutput, calls=%fused_computation.18.clone.1 | convolution fusion | flops 104857600 | bytes 229892 | tf_op jit(solution)/shard_map/while/body/eval_jaxpr/sc,fsb->cfb/dot_general | solution.py:16
  190.6 3.5 %fusion.53 = f32[16,12,4,256]{3,1,2,0:T(8,128)S(1)} fusion(f32[16,12,4,256]{3,1,2,0:T(8,128)S(1)} %get-tuple-element.287, s32[]{:T(128)S(6)} %copy.64, bf16[4096,12,1]{0,1,2:T(8,128)(2,1)S(1)} %reshape.526, bf16[256]{0:T(256)(128)(2,1)S(1)} %iota_convert_fusion.2, bf16[4,4096]{1,0:T(4,128)(2,1)S(1)} %dynamic-slice_bitcast_fusion.5), kind=kOutput, calls=%fused_computation.18.clone.1 | convolution fusion | flops 104857600 | bytes 229892 | tf_op jit(solution)/shard_map/while/body/eval_jaxpr/sc,fsb->cfb/dot_general | solution.py:16
  194.4 3.5 %fusion.53 = f32[16,12,4,256]{3,1,2,0:T(8,128)S(1)} fusion(f32[16,12,4,256]{3,1,2,0:T(8,128)S(1)} %get-tuple-element.287, s32[]{:T(128)S(6)} %copy.64, bf16[4096,12,1]{0,1,2:T(8,128)(2,1)S(1)} %reshape.526, bf16[256]{0:T(256)(128)(2,1)S(1)} %iota_convert_fusion.2, bf16[4,4096]{1,0:T(4,128)(2,1)S(1)} %dynamic-slice_bitcast_fusion.5), kind=kOutput, calls=%fused_computation.18.clone.1 | convolution fusion | flops 104857600 | bytes 229892 | tf_op jit(solution)/shard_map/while/body/eval_jaxpr/sc,fsb->cfb/dot_general | solution.py:16
  (197 shorter events, 84.1 us)
Async XLA Ops:
  7.2 216.2 %reduce-scatter.2.cloned.1.call-start = ((), (), s32[]{:S(2)}) async-start(), calls=%async_computation.3 | async-start | bytes 1769472 | tf_op jit(solution)/shard_map/reduce_scatter | solution.py:67
  48.9 0.7 copy-start.2
  48.9 1.4 copy-start.3
  48.9 2.1 copy-start.1
  48.9 20.3 %copy-start.4 = (s32[8]{0:T(128)S(1)}, s32[8]{0:T(128)}, u32[]{:S(2)}) copy-start(s32[8]{0:T(128)} %param.19) | copy-start | bytes 100
  48.9 21.0 %copy-start.5 = (s32[8]{0:T(128)S(1)}, s32[8]{0:T(128)}, u32[]{:S(2)}) copy-start(s32[8]{0:T(128)} %param.18) | copy-start | bytes 100
  48.9 46.0 %copy-start = (s32[2048,64]{0,1:T(8,128)S(1)}, s32[2048,64]{0,1:T(8,128)}, u32[]{:S(2)}) copy-start(s32[2048,64]{0,1:T(8,128)} %param.13) | copy-start | bytes 1572868
  127.4 13.3 %all-to-all-start.1 = ((bf16[4,8,512]{2,0,1:T(4,128)(2,1)}), bf16[4,8,512]{2,0,1:T(4,128)(2,1)S(1)}, u32[]{:S(2)}, u32[]{:S(2)}) async-start(bf16[4,8,512]{2,0,1:T(4,128)(2,1)} %copy.49), calls=%async_computation.2 | async-start | bytes 65536 | tf_op jit(solution)/shard_map/all_to_all | solution.py:84
  140.7 18.6 %all-to-all-start = ((bf16[64,8,512]{2,0,1:T(8,128)(2,1)}), bf16[64,8,512]{2,0,1:T(8,128)(2,1)S(1)}, u32[]{:S(2)}, u32[]{:S(2)}) async-start(bf16[64,8,512]{2,0,1:T(8,128)(2,1)} %copy.46), calls=%async_computation.1 | async-start | bytes 1048576 | tf_op jit(solution)/shard_map/all_to_all | solution.py:83
Sparse Core Ops, SparseCore 0:
  49.1 67.6 reduce-scatter.1
where the time goes:
time: 231 us; the launch traced here: 230 us
  matrix products  89.1 us (39%)
  other arithmetic  60.1 us (26%)
  local copies, waits for them, and re-layouts  28 us (12%)
  between operations  14.4 us (6%)
  blocking collectives  13.3 us (6%)
  waiting for transfers between devices  12.5 us (5%)
  starting transfers between devices  11.8 us (5%)
    dot_general x32, matrix products, one_block(): jnp.einsum('sc,fsb->cfb', weighted, table, preferred_element_type=jnp.flo...  89.1 us
    gather x3, other arithmetic, on_device(): child_feature[first_child + 1]  14.9 us
    gather x2, other arithmetic, on_device(): child_cutoff[first_child + 1]  14.6 us
    psum x1, blocking collectives, on_device(): lax.psum(picked.astype(jnp.float32), 'feat').astype(jnp.int32)  13.3 us
    all_to_all x1, waiting for transfers between devices, on_device(): lax.all_to_all(feat_buffer, 'rows', split_axis=1, concat_axis=1, tiled=True)  12.5 us
    gather x2, other arithmetic, on_device(): right_root = (split_values[0] > root_cutoff[tree_node]).astype(jnp.int32)  10 us
    scatter x1, local copies, waits for them, and re-layouts, on_device(): jnp.zeros((4, node_count * capacity), jnp.bfloat16).at[:, slot_index]  6.07 us
    scatter x1, local copies, waits for them, and re-layouts, on_device(): feat_buffer = jnp.zeros((feat_here, node_count * capacity), jnp.bfloat16)...  6.07 us
  transfers between devices with their start and end apart: 3, of which 1 were waited for; matrix products, arithmetic and copies ran while one was open for 59% of the time, Pallas kernels for 0%

commit v1 on v0

v1 whole, which is shorter than its diff:
```python
import functools

import jax
import jax.numpy as jnp
from jax import lax
from jax.experimental import pallas as pl
from jax.experimental.pallas import tpu as pltpu
from jax.sharding import PartitionSpec as P

BINS = 256
MESH = pl.DeviceIdType.MESH
NT = (((1,), (1,)), ((), ()))
EXTRA = 16


def exchange_kernel(
    owners,
    feat_devs,
    node_count,
    capacity,
    bins_ref,
    node_ref,
    units_ref,
    pick_ref,
    cut_ref,
    got_ref,
    pick_send,
    pick_recv,
    blocks,
    rows_in,
    slot_ref,
    pick_send_sem,
    pick_recv_sem,
    send_sem,
    recv_sem,
    self_sem,
):
    feat_here, rows_here = bins_ref.shape
    me = lax.axis_index("rows")
    mine = lax.axis_index("feat")

    barrier = pltpu.get_barrier_semaphore()
    for step in range(1, owners):
        pl.semaphore_signal(
            barrier, inc=1, device_id={"rows": lax.rem(me + step, owners)}, device_id_type=MESH
        )
    for step in range(1, feat_devs):
        pl.semaphore_signal(
            barrier, inc=1, device_id={"feat": lax.rem(mine + step, feat_devs)}, device_id_type=MESH
        )

    bins = bins_ref[...]
    node = node_ref[...]
    chosen = lax.broadcasted_iota(jnp.int32, (node_count, rows_here), 0) == node
    table = jnp.dot(pick_ref[...], bins, preferred_element_type=jnp.float32)
    picks, cuts = [], []
    for kind in range(3):
        part = table[kind * node_count : (kind + 1) * node_count]
        picks.append(jnp.sum(jnp.where(chosen, part, 0.0), axis=0, keepdims=True))
        limit = jnp.broadcast_to(cut_ref[:, kind : kind + 1], (node_count, rows_here))
        cuts.append(jnp.sum(jnp.where(chosen, limit, 0.0), axis=0, keepdims=True))
    picks.append(jnp.zeros_like(picks[0]))
    picks = jnp.concatenate(picks, axis=0)
    quarter = rows_here // 4
    folded = jnp.concatenate([picks[:, k * quarter : (k + 1) * quarter] for k in range(4)], axis=0)
    pick_send[...] = folded.astype(jnp.bfloat16)

    pl.semaphore_wait(barrier, owners - 1 + feat_devs - 1)

    pick_copies = []
    for step in range(1, feat_devs):
        copy = pltpu.make_async_remote_copy(
            src_ref=pick_send,
            dst_ref=pick_recv.at[step - 1],
            send_sem=pick_send_sem.at[step - 1],
            recv_sem=pick_recv_sem.at[step - 1],
            device_id={"feat": lax.rem(mine + step, feat_devs)},
            device_id_type=MESH,
        )
        copy.start()
        pick_copies.append(copy)

    chunk = 256
    ones = chosen.astype(jnp.float32)
    up_to = (
        lax.broadcasted_iota(jnp.int32, (chunk, chunk), 0)
        <= lax.broadcasted_iota(jnp.int32, (chunk, chunk), 1)
    ).astype(jnp.float32).astype(jnp.bfloat16)
    before = jnp.zeros((node_count, 1), jnp.float32)
    ranks = []
    for k in range(rows_here // chunk):
        here = ones[:, k * chunk : (k + 1) * chunk]
        counts = jnp.dot(here.astype(jnp.bfloat16), up_to, preferred_element_type=jnp.float32)
        counts = counts + before
        ranks.append(jnp.sum(here * counts, axis=0, keepdims=True))
        before = before + jnp.sum(here, axis=1, keepdims=True)
    rank = jnp.concatenate(ranks, axis=1).astype(jnp.int32) - 1
    slot_ref[...] = node * capacity + rank

    weight, treat, result = units_ref[0:1], units_ref[1:2], units_ref[2:3]
    scaled = weight * treat

    for copy in pick_copies:
        copy.wait()
    total = folded
    for step in range(feat_devs - 1):
        total = total + pick_recv[step].astype(jnp.float32)
    split = jnp.concatenate([total[4 * k : 4 * k + 4] for k in range(4)], axis=1)
    right_root = split[0:1] > cuts[0]
    first = jnp.where(split[1:2] > cuts[1], 1.0, 0.0)
    second = jnp.where(split[2:3] > cuts[2], 1.0, 0.0)
    leaf = jnp.where(right_root, 2.0 + second, first)
    extra = jnp.concatenate(
        [weight, scaled * treat, scaled * result, leaf, jnp.zeros((EXTRA - 4, rows_here), jnp.float32)],
        axis=0,
    ).astype(jnp.bfloat16)
    rows_in[0:feat_here] = bins
    rows_in[feat_here : feat_here + EXTRA] = extra

    place = lax.broadcasted_iota(jnp.int32, (capacity, rows_here), 0)

    def pack(owner):
        target = slot_ref[...] - owner * capacity
        here = jnp.where(place == target, 1.0, 0.0).astype(jnp.bfloat16)
        got = lax.dot_general(rows_in[...], here, NT, preferred_element_type=jnp.float32)
        blocks[owner] = got.astype(jnp.bfloat16)

    def send(step):
        owner = lax.rem(me + step, owners)
        return pltpu.make_async_remote_copy(
            src_ref=blocks.at[owner],
            dst_ref=got_ref.at[me],
            send_sem=send_sem.at[step - 1],
            recv_sem=recv_sem.at[step - 1],
            device_id={"rows": owner},
            device_id_type=MESH,
        )

    @pl.loop(1, owners)
    def _(step):
        pack(lax.rem(me + step, owners))
        send(step).start()

    pack(me)
    own = pltpu.make_async_copy(blocks.at[me], got_ref.at[me], self_sem)
    own.start()
    own.wait()

    @pl.loop(1, owners)
    def _(step):
        send(step).wait()


def histogram_kernel(got_ref, extra_ref, node_out, child_out, leaf_out):
    sources, group, capacity = got_ref.shape
    slots = sources * capacity
    bf = jnp.bfloat16
    extra = jnp.concatenate([extra_ref[s] for s in range(sources)], axis=1).astype(jnp.float32)
    row = lax.broadcasted_iota(jnp.int32, (16, slots), 0)
    kind = row % 3
    value = jnp.where(kind == 0, extra[0:1], jnp.where(kind == 1, extra[1:2], extra[2:3]))
    weights = jnp.where((row // 3).astype(jnp.float32) == extra[3:4], value, 0.0).astype(bf)
    bins = jnp.concatenate([got_ref[s] for s in range(sources)], axis=1).astype(jnp.float32)
    high = jnp.floor(bins * (1.0 / 64.0))
    low = (bins - 64.0 * high).astype(bf)
    high = high.astype(bf)
    level = lax.broadcasted_iota(jnp.int32, (16, slots), 0).astype(jnp.float32).astype(bf)
    one, zero = jnp.ones((), bf), jnp.zeros((), bf)
    lane = lax.broadcasted_iota(jnp.int32, (16, 128), 1)
    for base in range(0, group, 4):
        left, right = [], []
        for f in range(base, base + 4):
            high_f = jnp.broadcast_to(high[f : f + 1], (16, slots))
            low_f = jnp.broadcast_to(low[f : f + 1], (16, slots))
            for c in range(4):
                left.append(jnp.where(high_f == jnp.asarray(c, bf), weights, zero))
                right.append(jnp.where(low_f == level + jnp.asarray(16 * c, bf), one, zero))
        left = jnp.concatenate(left, axis=0)
        right = jnp.concatenate(right, axis=0)
        sums = lax.dot_general(left, right, NT, preferred_element_type=jnp.float32)
        for i in range(4):
            tile = 128 * (i // 2)
            parts = []
            for c in range(4):
                block = sums[64 * i + 16 * c : 64 * i + 16 * c + 16, tile : tile + 128]
                if c % 2 != i % 2:
                    block = pltpu.roll(block, 64, 1)
                parts.append(block)
            for t in range(2):
                full = jnp.where(lane < 64, parts[2 * t], parts[2 * t + 1])
                for q in range(4):
                    for m in range(3):
                        leaf_out[q, m, base + i : base + i + 1, 128 * t : 128 * t + 128] = full[
                            3 * q + m : 3 * q + m + 1
                        ]
    for m in range(3):
        a = leaf_out[0, m] + leaf_out[1, m]
        b = leaf_out[2, m] + leaf_out[3, m]
        child_out[0, m] = a
        child_out[1, m] = b
        node_out[0, m] = a + b


def on_device(
    owners,
    feat_devs,
    binned,
    node_index,
    treatment,
    outcome,
    unit_weight,
    root_feature,
    root_cutoff,
    child_feature,
    child_cutoff,
):
    rows_here, feat_here = binned.shape
    node_count = root_feature.shape[0]
    assert node_count == owners
    capacity = 2 * rows_here // node_count
    bf = jnp.bfloat16
    bins = binned.T.astype(bf)
    units = jnp.stack([unit_weight, treatment, outcome], 0)
    wanted = jnp.concatenate([root_feature, child_feature[0::2], child_feature[1::2]])
    wanted = wanted - lax.axis_index("feat") * feat_here
    pick = (wanted[:, None] == jnp.arange(feat_here)).astype(bf)
    cut = jnp.stack([root_cutoff, child_cutoff[0::2], child_cutoff[1::2]], 1).astype(jnp.float32)
    height = feat_here + EXTRA
    vmem = pl.BlockSpec(memory_space=pltpu.VMEM)
    dma = pltpu.SemaphoreType.DMA
    got = pl.pallas_call(
        functools.partial(exchange_kernel, owners, feat_devs, node_count, capacity),
        out_shape=jax.ShapeDtypeStruct((owners, height, capacity), bf),
        in_specs=[vmem] * 5,
        out_specs=pl.BlockSpec(memory_space=pl.ANY),
        scratch_shapes=[
            pltpu.VMEM((16, rows_here // 4), bf),
            pltpu.VMEM((feat_devs - 1, 16, rows_here // 4), bf),
            pltpu.VMEM((owners, height, capacity), bf),
            pltpu.VMEM((height, rows_here), bf),
            pltpu.VMEM((1, rows_here), jnp.int32),
            dma((feat_devs - 1,)),
            dma((feat_devs - 1,)),
            dma((owners - 1,)),
            dma((owners - 1,)),
            dma,
        ],
        compiler_params=pltpu.CompilerParams(
            collective_id=0, has_side_effects=True, vmem_limit_bytes=48 * 1024 * 1024
        ),
        name="exchange",
    )(bins, node_index.reshape(1, rows_here), units, pick, cut)

    group = 16
    return pl.pallas_call(
        histogram_kernel,
        grid=(feat_here // group,),
        out_shape=tuple(
            jax.ShapeDtypeStruct((k, 3, feat_here, BINS), jnp.float32) for k in (1, 2, 4)
        ),
        in_specs=[
            pl.BlockSpec((owners, group, capacity), lambda i: (0, i, 0)),
            pl.BlockSpec((owners, EXTRA, capacity), lambda i: (0, feat_here // EXTRA, 0)),
        ],
        out_specs=tuple(pl.BlockSpec((k, 3, group, BINS), lambda i: (0, 0, i, 0)) for k in (1, 2, 4)),
        compiler_params=pltpu.CompilerParams(vmem_limit_bytes=48 * 1024 * 1024),
        name="histogram",
    )(got, got)


def solution(mesh):
    in_specs = (
        P("rows", "feat"),
        P("rows", None),
        P("rows"),
        P("rows"),
        P("rows"),
        P(),
        P(),
        P(),
        P(),
    )
    out_specs = (P("rows", None, "feat", None),) * 3
    body = functools.partial(on_device, mesh.shape["rows"], mesh.shape["feat"])
    return jax.shard_map(body, mesh=mesh, in_specs=in_specs, out_specs=out_specs, check_vma=False)
```

time: 231 us -> 41.4 us (0.18)
  the two profiles are of different devices: /device:TPU:0 before, /device:TPU:11 now
where the time goes in v1:
time: 41.4 us; the launch traced here: 41 us
  Pallas kernels  35.5 us (86%)
  local copies, waits for them, and re-layouts  3.57 us (9%)
  other arithmetic  1.33 us (3%)
  between operations  0.68 us (2%)
    pallas_call x1, Pallas kernels, on_device(): pl.pallas_call(functools.partial(exchange_kernel, owners, feat_devs, node...  24.4 us
    pallas_call x1, Pallas kernels, on_device(): pl.pallas_call(histogram_kernel, grid=(feat_here // group,), out_shape=tu...  11 us
    unnamed x16, local copies, waits for them, and re-layouts  2.94 us
    convert_element_type x1, other arithmetic, on_device(): bins = binned.T.astype(bf)  1.08 us

profile of v1, /device:TPU:11, one launch (start us, length us, event | category | flops | bytes accessed | tf_op | source)
XLA Modules:
  0.0 41.0 jit_solution(2440336243347939335)
XLA Ops:
  0.6 0.0 copy-start.6
  0.6 0.6 %copy-done.6 = s32[16]{0:T(128)S(1)} copy-done((s32[16]{0:T(128)S(1)}, s32[16]{0:T(128)}, u32[]{:S(2)}) %copy-start.6) | copy-done | bytes 88
  1.3 0.1 slice.13
  1.4 0.0 copy-start.4
  1.4 0.1 slice.12
  1.5 0.6 %copy-done.4 = s32[8]{0:T(128)S(1)} copy-done((s32[8]{0:T(128)S(1)}, s32[8]{0:T(128)}, u32[]{:S(2)}) %copy-start.4) | copy-done | bytes 56
  2.0 0.1 add_subtract_fusion
  2.1 0.6 %copy-done.7 = s32[16]{0:T(128)S(1)} copy-done((s32[16]{0:T(128)S(1)}, s32[16]{0:T(128)}, u32[]{:S(2)}) %copy-start.7) | copy-done | bytes 88
  2.7 0.1 slice.15
  2.8 0.1 slice.14
  2.9 0.1 copy.13
  3.0 0.1 copy.14
  3.1 0.6 %copy-done.5 = s32[8]{0:T(128)S(1)} copy-done((s32[8]{0:T(128)S(1)}, s32[8]{0:T(128)}, u32[]{:S(2)}) %copy-start.5) | copy-done | bytes 56
  3.6 0.1 copy.12
  3.7 0.1 add_convert_fusion.cut_ref
  3.8 0.1 fusion.pick_ref
  3.9 0.5 %copy-done.3 = f32[2048]{0:T(1024)S(1)} copy-done((f32[2048]{0:T(1024)S(1)}, f32[2048]{0:T(1024)}, u32[]{:S(2)}) %copy-start.3) | copy-done | bytes 8216
  4.3 0.1 copy-done.1
  4.4 0.0 copy-done.2
  4.5 0.0 copy-start
  4.5 1.1 %convert_bitcast_fusion.bins_ref = bf16[64,2048]{1,0:T(8,128)(2,1)S(1)} fusion(s32[2048,64]{0,1:T(8,128)} %param.9), kind=kLoop, calls=%fused_computation | loop fusion | flops 131072 | bytes 786432 | tf_op jit(solution)/shard_map/convert_element_type | solution.py:222
  5.6 0.0 copy-done
  5.6 24.4 %exchange.1.got_ref.extra_ref = bf16[8,80,512]{2,1,0:T(8,128)(2,1)S(1)} custom-call(bf16[64,2048]{1,0:T(8,128)(2,1)S(1)} %convert_bitcast_fusion.bins_ref, s32[1,2048]{1,0:T(1,128)S(1)} %bitcast.9, f32[3,2048]{1,0:T(4,128)S(1)} %pad_maximum_fusion.units_ref, bf16[24,64]{1,0:T(8,128)(2,1)S(1)} %fusion.pick_ref, f32[8,3]{1,0:T(8,128)S(1)} %add_convert_fusion.cut_ref), custom_call_target="tpu_custom_call" | custom-call | tf_op jit(solution)/shard_map/exchange/pallas_call | solution.py:231
  30.0 11.0 %histogram.1 = (f32[1,3,64,256]{3,2,1,0:T(8,128)}, f32[2,3,64,256]{3,2,1,0:T(8,128)}, f32[4,3,64,256]{3,2,1,0:T(8,128)}) custom-call(bf16[8,80,512]{2,1,0:T(8,128)(2,1)S(1)} %exchange.1.got_ref.extra_ref, bf16[8,80,512]{2,1,0:T(8,128)(2,1)S(1)} %exchange.1.got_ref.extra_ref), custom_call_target="tpu_custom_call" | custom-call | tf_op jit(solution)/shard_map/histogram/pallas_call | solution.py:255
  (6 shorter events, 0.0 us)
Async XLA Ops:
  0.6 0.7 %copy-start.6 = (s32[16]{0:T(128)S(1)}, s32[16]{0:T(128)}, u32[]{:S(2)}) copy-start(s32[16]{0:T(128)} %param.16) | copy-start | bytes 196
  1.4 0.7 %copy-start.4 = (s32[8]{0:T(128)S(1)}, s32[8]{0:T(128)}, u32[]{:S(2)}) copy-start(s32[8]{0:T(128)} %param.14) | copy-start | bytes 100
  2.0 0.7 %copy-start.7 = (s32[16]{0:T(128)S(1)}, s32[16]{0:T(128)}, u32[]{:S(2)}) copy-start(s32[16]{0:T(128)} %param.17) | copy-start | bytes 196
  3.0 0.7 %copy-start.5 = (s32[8]{0:T(128)S(1)}, s32[8]{0:T(128)}, u32[]{:S(2)}) copy-start(s32[8]{0:T(128)} %param.15) | copy-start | bytes 100
  3.6 0.7 %copy-start.3 = (f32[2048]{0:T(1024)S(1)}, f32[2048]{0:T(1024)}, u32[]{:S(2)}) copy-start(f32[2048]{0:T(1024)} %param.13) | copy-start | bytes 24580
  3.7 0.7 %copy-start.1 = (f32[2048]{0:T(1024)S(1)}, f32[2048]{0:T(1024)}, u32[]{:S(2)}) copy-start(f32[2048]{0:T(1024)} %param.12) | copy-start | bytes 24580
  3.7 0.7 %copy-start.2 = (f32[2048]{0:T(1024)S(1)}, f32[2048]{0:T(1024)}, u32[]{:S(2)}) copy-start(f32[2048]{0:T(1024)} %param.11) | copy-start | bytes 24580
  4.5 1.1 %copy-start = (s32[2048,1]{0,1:T(1,128)S(1)}, s32[2048,1]{0,1:T(1,128)}, u32[]{:S(2)}) copy-start(s32[2048,1]{0,1:T(1,128)} %param.10) | copy-start | bytes 24580

commit v2 on v1

v2 whole, which is shorter than its diff:
```python
import functools

import jax
import jax.numpy as jnp
from jax import lax
from jax.experimental import pallas as pl
from jax.experimental.pallas import tpu as pltpu
from jax.sharding import PartitionSpec as P

BINS = 256
MESH = pl.DeviceIdType.MESH
NT = (((1,), (1,)), ((), ()))
EXTRA = 16
CHUNKS = 4
GROUP = 16
AHEAD = 4


def partner_of(me, step, owners):
    total, bit = 0, 1
    while bit < owners:
        total = total + lax.rem(me // bit + step // bit, 2) * bit
        bit *= 2
    return total


def weight_rows(extra):
    slots = extra.shape[1]
    row = lax.broadcasted_iota(jnp.int32, (16, slots), 0)
    kind = row % 3
    value = jnp.where(kind == 0, extra[0:1], jnp.where(kind == 1, extra[1:2], extra[2:3]))
    same = (row // 3).astype(jnp.float32) == extra[3:4]
    return jnp.where(same, value, 0.0).astype(jnp.bfloat16)


def pair_sums(bins, weights):
    slots = bins.shape[1]
    bf = jnp.bfloat16
    high = jnp.floor(bins * (1.0 / 64.0))
    low = (bins - 64.0 * high).astype(bf)
    high = high.astype(bf)
    level = lax.broadcasted_iota(jnp.int32, (16, slots), 0).astype(jnp.float32).astype(bf)
    one, zero = jnp.ones((), bf), jnp.zeros((), bf)
    lane = lax.broadcasted_iota(jnp.int32, (64, 128), 1)
    pairs = []
    for base in range(0, GROUP, 4):
        left, right = [], []
        for f in range(base, base + 4):
            high_f = jnp.broadcast_to(high[f : f + 1], (16, slots))
            low_f = jnp.broadcast_to(low[f : f + 1], (16, slots))
            for c in range(4):
                left.append(jnp.where(high_f == jnp.asarray(c, bf), weights, zero))
                right.append(jnp.where(low_f == level + jnp.asarray(16 * c, bf), one, zero))
        left = jnp.concatenate(left, axis=0)
        right = jnp.concatenate(right, axis=0)
        sums = lax.dot_general(left, right, NT, preferred_element_type=jnp.float32)
        for i in range(2):
            even = sums[128 * i : 128 * i + 64, 128 * i : 128 * i + 128]
            odd = sums[128 * i + 64 : 128 * i + 128, 128 * i : 128 * i + 128]
            pairs.append(jnp.where(lane < 64, even, odd))
    return pairs


def exchange_kernel(
    owners,
    feat_devs,
    node_count,
    capacity,
    bins_hbm,
    node_hbm,
    weight_hbm,
    treat_hbm,
    result_hbm,
    root_feat_hbm,
    root_cut_hbm,
    child_feat_hbm,
    child_cut_hbm,
    late_ref,
    acc_ref,
    bins_in,
    node_in,
    weight_in,
    treat_in,
    result_in,
    root_feat_in,
    root_cut_in,
    child_feat_in,
    child_cut_in,
    pick_send,
    pick_recv,
    blocks,
    got,
    rows_in,
    slot_ref,
    places,
    weights_ref,
    in_sem,
    pick_send_sem,
    pick_recv_sem,
    send_sem,
    recv_sem,
):
    feat_here, rows_here = bins_in.shape
    me = lax.axis_index("rows")
    mine = lax.axis_index("feat")
    bf = jnp.bfloat16

    pairs = [
        (node_hbm, node_in),
        (bins_hbm, bins_in),
        (root_feat_hbm, root_feat_in),
        (child_feat_hbm, child_feat_in),
        (root_cut_hbm, root_cut_in),
        (child_cut_hbm, child_cut_in),
        (weight_hbm, weight_in),
        (treat_hbm, treat_in),
        (result_hbm, result_in),
    ]
    loads = [pltpu.make_async_copy(a, b, in_sem.at[k]) for k, (a, b) in enumerate(pairs)]
    for load in loads:
        load.start()

    barrier = pltpu.get_barrier_semaphore()
    for step in range(1, owners):
        pl.semaphore_signal(
            barrier,
            inc=1,
            device_id={"rows": partner_of(me, step, owners)},
            device_id_type=MESH,
        )
    for step in range(1, feat_devs):
        pl.semaphore_signal(
            barrier, inc=1, device_id={"feat": lax.rem(mine + step, feat_devs)}, device_id_type=MESH
        )

    for load in loads:
        load.wait()
    node = node_in[...]
    bins = bins_in[...].astype(jnp.float32).astype(bf)
    rows_in[0:feat_here] = bins
    chosen = lax.broadcasted_iota(jnp.int32, (node_count, rows_here), 0) == node

    def column(table, stride, first):
        width = table.shape[1]
        spot = lax.broadcasted_iota(jnp.int32, (node_count, width), 0) * stride + first
        lane = lax.broadcasted_iota(jnp.int32, (node_count, width), 1)
        picked = jnp.where(lane == spot, table.astype(jnp.float32), 0.0)
        return jnp.sum(picked, axis=1, keepdims=True)

    wanted = [
        column(root_feat_in[...], 1, 0),
        column(child_feat_in[...], 2, 0),
        column(child_feat_in[...], 2, 1),
    ]
    limits = [
        column(root_cut_in[...], 1, 0),
        column(child_cut_in[...], 2, 0),
        column(child_cut_in[...], 2, 1),
    ]
    local = lax.broadcasted_iota(jnp.int32, (node_count, feat_here), 1) + mine * feat_here
    local = local.astype(jnp.float32)
    pick = jnp.concatenate([jnp.where(local == w, 1.0, 0.0) for w in wanted], axis=0).astype(bf)
    table = jnp.dot(pick, bins, preferred_element_type=jnp.float32)
    picks, cuts = [], []
    for kind in range(3):
        part = table[kind * node_count : (kind + 1) * node_count]
        picks.append(jnp.sum(jnp.where(chosen, part, 0.0), axis=0, keepdims=True))
        limit = jnp.broadcast_to(limits[kind], (node_count, rows_here))
        cuts.append(jnp.sum(jnp.where(chosen, limit, 0.0), axis=0, keepdims=True))
    picks.append(jnp.zeros_like(picks[0]))
    picks = jnp.concatenate(picks, axis=0)
    quarter = rows_here // 4
    folded = jnp.concatenate([picks[:, k * quarter : (k + 1) * quarter] for k in range(4)], axis=0)
    pick_send[...] = folded.astype(bf)

    pl.semaphore_wait(barrier, owners - 1 + feat_devs - 1)

    pick_copies = []
    for step in range(1, feat_devs):
        copy = pltpu.make_async_remote_copy(
            src_ref=pick_send,
            dst_ref=pick_recv.at[step - 1],
            send_sem=pick_send_sem.at[step - 1],
            recv_sem=pick_recv_sem.at[step - 1],
            device_id={"feat": lax.rem(mine + step, feat_devs)},
            device_id_type=MESH,
        )
        copy.start()
        pick_copies.append(copy)

    chunk = 256
    ones = chosen.astype(jnp.float32)
    up_to = lax.broadcasted_iota(jnp.int32, (chunk, chunk), 0) <= lax.broadcasted_iota(
        jnp.int32, (chunk, chunk), 1
    )
    up_to = up_to.astype(jnp.float32).astype(bf)
    before = jnp.zeros((node_count, 1), jnp.float32)
    ranks = []
    for k in range(rows_here // chunk):
        here = ones[:, k * chunk : (k + 1) * chunk]
        counts = jnp.dot(here.astype(bf), up_to, preferred_element_type=jnp.float32) + before
        ranks.append(jnp.sum(here * counts, axis=0, keepdims=True))
        before = before + jnp.sum(here, axis=1, keepdims=True)
    rank = jnp.concatenate(ranks, axis=1).astype(jnp.int32) - 1
    slot_ref[...] = node * capacity + rank

    weight, treat, result = weight_in[...], treat_in[...], result_in[...]
    scaled = weight * treat
    place = lax.broadcasted_iota(jnp.int32, (capacity, rows_here), 0)

    def fill(step, where):
        target = slot_ref[...] - partner_of(me, step, owners) * capacity
        places[where] = jnp.where(place == target, 1.0, 0.0).astype(bf)

    half = owners // 2

    @pl.loop(0, AHEAD)
    def _(k):
        fill(half + k, k)

    for copy in pick_copies:
        copy.wait()
    total = folded
    for step in range(feat_devs - 1):
        total = total + pick_recv[step].astype(jnp.float32)
    split = jnp.concatenate([total[4 * k : 4 * k + 4] for k in range(4)], axis=1)
    right_root = split[0:1] > cuts[0]
    first = jnp.where(split[1:2] > cuts[1], 1.0, 0.0)
    second = jnp.where(split[2:3] > cuts[2], 1.0, 0.0)
    leaf = jnp.where(right_root, 2.0 + second, first)
    none = jnp.zeros((EXTRA - 4, rows_here), jnp.float32)
    extra = jnp.concatenate([weight, scaled * treat, scaled * result, leaf, none], axis=0)
    rows_in[feat_here : feat_here + EXTRA] = extra.astype(bf)

    def packed(where):
        moved = lax.dot_general(rows_in[...], places[where], NT, preferred_element_type=jnp.float32)
        return moved.astype(bf)

    per = owners // CHUNKS
    late_first = owners - per

    def send(step, late):
        place_there = late_ref.at[step - late_first] if late else got.at[step]
        return pltpu.make_async_remote_copy(
            src_ref=blocks.at[step],
            dst_ref=place_there,
            send_sem=send_sem.at[step],
            recv_sem=recv_sem.at[step],
            device_id={"rows": partner_of(me, step, owners)},
            device_id_type=MESH,
        )

    def each(start, stop, late, prepared):
        @pl.loop(start, stop)
        def _(step):
            where = lax.rem(step, AHEAD)
            if not prepared:
                fill(step, where)
            blocks[step] = packed(where)
            send(step, late).start()

    early = half + AHEAD
    for start, stop, prepared in ((half, early, True), (early, owners, False)):
        if start < min(stop, late_first):
            each(start, min(stop, late_first), False, prepared)
        if max(start, late_first) < stop:
            each(max(start, late_first), stop, True, prepared)
    while half > 1:
        half //= 2
        each(half, 2 * half, False, False)
    fill(0, 0)
    got[0] = packed(0)

    for c in range(CHUNKS - 1):
        for step in range(max(1, c * per), (c + 1) * per):
            send(step, False).wait_recv()
        known = got[c * per : (c + 1) * per, feat_here : feat_here + EXTRA]
        known = jnp.concatenate([known[s] for s in range(per)], axis=1).astype(jnp.float32)
        weights_ref[...] = weight_rows(known)

        @pl.loop(0, feat_here // GROUP)
        def _(block):
            rows = pl.ds(pl.multiple_of(block * GROUP, GROUP), GROUP)
            values = jnp.concatenate([got[c * per + s, rows] for s in range(per)], axis=1)
            sums = pair_sums(values.astype(jnp.float32), weights_ref[...])
            for k, part in enumerate(sums):
                spot = block * (GROUP // 2) + k
                acc_ref[spot] = part if c == 0 else acc_ref[spot] + part

    for step in range(1, owners):
        send(step, step >= late_first).wait_send()
    for step in range(late_first, owners):
        send(step, True).wait_recv()


def finish_kernel(late_ref, extra_ref, acc_ref, node_out, child_out, leaf_out):
    sources = late_ref.shape[0]
    extra = jnp.concatenate([extra_ref[s] for s in range(sources)], axis=1).astype(jnp.float32)
    bins = jnp.concatenate([late_ref[s] for s in range(sources)], axis=1).astype(jnp.float32)
    lane = lax.broadcasted_iota(jnp.int32, (16, 128), 1)
    for k, part in enumerate(pair_sums(bins, weight_rows(extra))):
        part = part + acc_ref[k]
        parts = [part[16 * c : 16 * c + 16] for c in range(4)]
        turned = [pltpu.roll(p, 64, 1) for p in parts]
        for i in range(2):
            f = 2 * k + i
            for t in range(2):
                if i == 0:
                    full = jnp.where(lane < 64, parts[2 * t], turned[2 * t + 1])
                else:
                    full = jnp.where(lane < 64, turned[2 * t], parts[2 * t + 1])
                for q in range(4):
                    for m in range(3):
                        leaf_out[q, m, f : f + 1, 128 * t : 128 * t + 128] = full[
                            3 * q + m : 3 * q + m + 1
                        ]
    for m in range(3):
        a = leaf_out[0, m] + leaf_out[1, m]
        b = leaf_out[2, m] + leaf_out[3, m]
        child_out[0, m] = a
        child_out[1, m] = b
        node_out[0, m] = a + b


def on_device(
    owners,
    feat_devs,
    binned,
    node_index,
    treatment,
    outcome,
    unit_weight,
    root_feature,
    root_cutoff,
    child_feature,
    child_cutoff,
):
    rows_here, feat_here = binned.shape
    node_count = root_feature.shape[0]
    assert node_count == owners and owners >= 2 * AHEAD and owners & (owners - 1) == 0
    capacity = 2 * rows_here // node_count
    bf, f32, i32 = jnp.bfloat16, jnp.float32, jnp.int32
    height = feat_here + EXTRA
    per = owners // CHUNKS
    dma = pltpu.SemaphoreType.DMA
    anywhere = pl.BlockSpec(memory_space=pltpu.HBM)
    vmem = pl.BlockSpec(memory_space=pltpu.VMEM)
    late, acc = pl.pallas_call(
        functools.partial(exchange_kernel, owners, feat_devs, node_count, capacity),
        out_shape=(
            jax.ShapeDtypeStruct((per, height, capacity), bf),
            jax.ShapeDtypeStruct((feat_here // 2, 64, 128), f32),
        ),
        in_specs=[anywhere] * 9,
        out_specs=(anywhere, vmem),
        scratch_shapes=[
            pltpu.VMEM((feat_here, rows_here), i32),
            pltpu.VMEM((1, rows_here), i32),
            pltpu.VMEM((1, rows_here), f32),
            pltpu.VMEM((1, rows_here), f32),
            pltpu.VMEM((1, rows_here), f32),
            pltpu.VMEM((1, node_count), i32),
            pltpu.VMEM((1, node_count), i32),
            pltpu.VMEM((1, 2 * node_count), i32),
            pltpu.VMEM((1, 2 * node_count), i32),
            pltpu.VMEM((16, rows_here // 4), bf),
            pltpu.VMEM((feat_devs - 1, 16, rows_here // 4), bf),
            pltpu.VMEM((owners, height, capacity), bf),
            pltpu.VMEM((owners - per, height, capacity), bf),
            pltpu.VMEM((height, rows_here), bf),
            pltpu.VMEM((1, rows_here), i32),
            pltpu.VMEM((AHEAD, capacity, rows_here), bf),
            pltpu.VMEM((16, per * capacity), bf),
            dma((9,)),
            dma((feat_devs - 1,)),
            dma((feat_devs - 1,)),
            dma((owners,)),
            dma((owners,)),
        ],
        compiler_params=pltpu.CompilerParams(
            collective_id=0, has_side_effects=True, vmem_limit_bytes=64 * 1024 * 1024
        ),
        name="exchange",
    )(
        binned.T,
        node_index.reshape(1, rows_here),
        unit_weight.reshape(1, rows_here),
        treatment.reshape(1, rows_here),
        outcome.reshape(1, rows_here),
        root_feature.reshape(1, node_count),
        root_cutoff.reshape(1, node_count),
        child_feature.reshape(1, 2 * node_count),
        child_cutoff.reshape(1, 2 * node_count),
    )

    return pl.pallas_call(
        finish_kernel,
        grid=(feat_here // GROUP,),
        out_shape=tuple(
            jax.ShapeDtypeStruct((k, 3, feat_here, BINS), f32) for k in (1, 2, 4)
        ),
        in_specs=[
            pl.BlockSpec((per, GROUP, capacity), lambda i: (0, i, 0)),
            pl.BlockSpec((per, EXTRA, capacity), lambda i: (0, feat_here // EXTRA, 0)),
            pl.BlockSpec((GROUP // 2, 64, 128), lambda i: (i, 0, 0)),
        ],
        out_specs=tuple(pl.BlockSpec((k, 3, GROUP, BINS), lambda i: (0, 0, i, 0)) for k in (1, 2, 4)),
        compiler_params=pltpu.CompilerParams(vmem_limit_bytes=64 * 1024 * 1024),
        name="finish",
    )(late, late, acc)


def solution(mesh):
    in_specs = (
        P("rows", "feat"),
        P("rows", None),
        P("rows"),
        P("rows"),
        P("rows"),
        P(),
        P(),
        P(),
        P(),
    )
    out_specs = (P("rows", None, "feat", None),) * 3
    body = functools.partial(on_device, mesh.shape["rows"], mesh.shape["feat"])
    return jax.shard_map(body, mesh=mesh, in_specs=in_specs, out_specs=out_specs, check_vma=False)
```

time: 41.4 us -> 39.5 us (0.954)
  the two profiles are of different devices: /device:TPU:11 before, /device:TPU:0 now
where the time goes in v2:
time: 39.5 us; the launch traced here: 39.2 us
  Pallas kernels  38.6 us (98%)
  between operations  0.64 us (2%)
    pallas_call x1, Pallas kernels, on_device(): pl.pallas_call(functools.partial(exchange_kernel, owners, feat_devs, node...  32.9 us
    pallas_call x1, Pallas kernels, on_device(): pl.pallas_call(finish_kernel, grid=(feat_here // GROUP,), out_shape=tuple...  5.7 us

profile of v2, /device:TPU:0, one launch (start us, length us, event | category | flops | bytes accessed | tf_op | source)
XLA Modules:
  0.0 39.2 jit_solution(7205946024375932118)
XLA Ops:
  0.6 32.9 %exchange.1 = (bf16[2,80,512]{2,1,0:T(8,128)(2,1)}, f32[32,64,128]{2,1,0:T(8,128)}) custom-call(s32[64,2048]{1,0:T(8,128)} %bitcast.9, s32[1,2048]{1,0:T(1,128)} %bitcast.10, f32[1,2048]{1,0:T(1,128)} %bitcast.11, f32[1,2048]{1,0:T(1,128)} %bitcast.12, f32[1,2048]{1,0:T(1,128)} %bitcast.13, s32[1,8]{1,0:T(1,128)} %bitcast.14, s32[1,8]{1,0:T(1,128)} %bitcast.15, ...), custom_call_target="tpu_custom_call" | custom-call | tf_op jit(solution)/shard_map/exchange/pallas_call | solution.py:348
  33.5 5.7 %finish.1 = (f32[1,3,64,256]{3,2,1,0:T(8,128)}, f32[2,3,64,256]{3,2,1,0:T(8,128)}, f32[4,3,64,256]{3,2,1,0:T(8,128)}) custom-call(bf16[2,80,512]{2,1,0:T(8,128)(2,1)} %get-tuple-element.5.late_ref.extra_ref, bf16[2,80,512]{2,1,0:T(8,128)(2,1)} %get-tuple-element.5.late_ref.extra_ref, f32[32,64,128]{2,1,0:T(8,128)} %get-tuple-element.6.acc_ref), custom_call_target="tpu_custom_call" | custom-call | tf_op jit(solution)/shard_map/finish/pallas_call | solution.py:396

commit v3 on v2

--- a/solution.py
+++ b/solution.py
@@ -13,7 +13,7 @@
 EXTRA = 16
 CHUNKS = 4
 GROUP = 16
-AHEAD = 4
+LANES = 128
 
 
 def partner_of(me, step, owners):
@@ -22,6 +22,20 @@
         total = total + lax.rem(me // bit + step // bit, 2) * bit
         bit *= 2
     return total
+
+
+def fold(extra):
+    parts = extra.shape[1] // LANES
+    pieces = [extra[0:4, k * LANES : (k + 1) * LANES] for k in range(parts)]
+    if parts < 4:
+        pieces.append(jnp.zeros((EXTRA - 4 * parts, LANES), extra.dtype))
+    return jnp.concatenate(pieces, axis=0)
+
+
+def unfold(folded, capacity):
+    folded = folded.astype(jnp.float32)
+    parts = [folded[4 * k : 4 * k + 4] for k in range(capacity // LANES)]
+    return jnp.concatenate(parts, axis=1)
 
 
 def weight_rows(extra):
@@ -76,6 +90,7 @@
     child_feat_hbm,
     child_cut_hbm,
     late_ref,
+    late_extra_ref,
     acc_ref,
     bins_in,
     node_in,
@@ -89,8 +104,11 @@
     pick_send,
     pick_recv,
     blocks,
+    extra_blocks,
     got,
-    rows_in,
+    got_extra,
+    bins_rows,
+    extra_rows,
     slot_ref,
     places,
     weights_ref,
@@ -99,6 +117,8 @@
     pick_recv_sem,
     send_sem,
     recv_sem,
+    extra_send_sem,
+    extra_recv_sem,
 ):
     feat_here, rows_here = bins_in.shape
     me = lax.axis_index("rows")
@@ -137,7 +157,7 @@
         load.wait()
     node = node_in[...]
     bins = bins_in[...].astype(jnp.float32).astype(bf)
-    rows_in[0:feat_here] = bins
+    bins_rows[...] = bins
     chosen = lax.broadcasted_iota(jnp.int32, (node_count, rows_here), 0) == node
 
     def column(table, stride, first):
@@ -204,20 +224,60 @@
     rank = jnp.concatenate(ranks, axis=1).astype(jnp.int32) - 1
     slot_ref[...] = node * capacity + rank
 
+    half = owners // 2
+    per = owners // CHUNKS
+    late_first = owners - per
+    block = min(256, capacity)
+    level = lax.broadcasted_iota(jnp.int32, (16, rows_here), 0).astype(jnp.float32).astype(bf)
+    one, zero = jnp.ones((), bf), jnp.zeros((), bf)
+
+    def fill(step, where):
+        target = slot_ref[...] - partner_of(me, step, owners) * capacity
+        for start in range(0, capacity, block):
+            inside = target - start
+            inside = jnp.where((inside >= 0) & (inside < block), inside, -1)
+            inside = inside.astype(jnp.float32).astype(bf)
+            inside = jnp.broadcast_to(inside, (16, rows_here))
+            for k in range(0, block, 16):
+                places[where, start + k : start + k + 16] = jnp.where(
+                    inside == level + jnp.asarray(k, bf), one, zero
+                )
+
+    def moved(rows_ref, where):
+        return lax.dot_general(
+            rows_ref[...], places[where], NT, preferred_element_type=jnp.float32
+        )
+
+    def send(step, late):
+        return pltpu.make_async_remote_copy(
+            src_ref=blocks.at[step],
+            dst_ref=late_ref.at[step - late_first] if late else got.at[step],
+            send_sem=send_sem.at[step],
+            recv_sem=recv_sem.at[step],
+            device_id={"rows": partner_of(me, step, owners)},
+            device_id_type=MESH,
+        )
+
+    def send_extra(step, late):
+        return pltpu.make_async_remote_copy(
+            src_ref=extra_blocks.at[step],
+            dst_ref=late_extra_ref.at[step - late_first] if late else got_extra.at[step],
+            send_sem=extra_send_sem.at[step],
+            recv_sem=extra_recv_sem.at[step],
+            device_id={"rows": partner_of(me, step, owners)},
+            device_id_type=MESH,
+        )
+
+    for start, stop, late in ((half, late_first, False), (late_first, owners, True)):
+
+        @pl.loop(start, stop)
+        def _(step):
+            fill(step, step - half)
+            blocks[step] = moved(bins_rows, step - half).astype(bf)
+            send(step, late).start()
+
     weight, treat, result = weight_in[...], treat_in[...], result_in[...]
     scaled = weight * treat
-    place = lax.broadcasted_iota(jnp.int32, (capacity, rows_here), 0)
-
-    def fill(step, where):
-        target = slot_ref[...] - partner_of(me, step, owners) * capacity
-        places[where] = jnp.where(place == target, 1.0, 0.0).astype(bf)
-
-    half = owners // 2
-
-    @pl.loop(0, AHEAD)
-    def _(k):
-        fill(half + k, k)
-
     for copy in pick_copies:
         copy.wait()
     total = folded
@@ -230,52 +290,34 @@
     leaf = jnp.where(right_root, 2.0 + second, first)
     none = jnp.zeros((EXTRA - 4, rows_here), jnp.float32)
     extra = jnp.concatenate([weight, scaled * treat, scaled * result, leaf, none], axis=0)
-    rows_in[feat_here : feat_here + EXTRA] = extra.astype(bf)
-
-    def packed(where):
-        moved = lax.dot_general(rows_in[...], places[where], NT, preferred_element_type=jnp.float32)
-        return moved.astype(bf)
-
-    per = owners // CHUNKS
-    late_first = owners - per
-
-    def send(step, late):
-        place_there = late_ref.at[step - late_first] if late else got.at[step]
-        return pltpu.make_async_remote_copy(
-            src_ref=blocks.at[step],
-            dst_ref=place_there,
-            send_sem=send_sem.at[step],
-            recv_sem=recv_sem.at[step],
-            device_id={"rows": partner_of(me, step, owners)},
-            device_id_type=MESH,
-        )
-
-    def each(start, stop, late, prepared):
+    extra_rows[...] = extra.astype(bf)
+
+    for start, stop, late in ((half, late_first, False), (late_first, owners, True)):
+
         @pl.loop(start, stop)
         def _(step):
-            where = lax.rem(step, AHEAD)
-            if not prepared:
-                fill(step, where)
-            blocks[step] = packed(where)
-            send(step, late).start()
-
-    early = half + AHEAD
-    for start, stop, prepared in ((half, early, True), (early, owners, False)):
-        if start < min(stop, late_first):
-            each(start, min(stop, late_first), False, prepared)
-        if max(start, late_first) < stop:
-            each(max(start, late_first), stop, True, prepared)
-    while half > 1:
-        half //= 2
-        each(half, 2 * half, False, False)
+            extra_blocks[step] = fold(moved(extra_rows, step - half)).astype(bf)
+            send_extra(step, late).start()
+
+    @pl.loop(1, half)
+    def _(back):
+        step = half - back
+        fill(step, step)
+        blocks[step] = moved(bins_rows, step).astype(bf)
+        send(step, False).start()
+        extra_blocks[step] = fold(moved(extra_rows, step)).astype(bf)
+        send_extra(step, False).start()
+
     fill(0, 0)
-    got[0] = packed(0)
+    got[0] = moved(bins_rows, 0).astype(bf)
+    got_extra[0] = fold(moved(extra_rows, 0)).astype(bf)
 
     for c in range(CHUNKS - 1):
         for step in range(max(1, c * per), (c + 1) * per):
             send(step, False).wait_recv()
-        known = got[c * per : (c + 1) * per, feat_here : feat_here + EXTRA]
-        known = jnp.concatenate([known[s] for s in range(per)], axis=1).astype(jnp.float32)
+            send_extra(step, False).wait_recv()
+        known = [unfold(got_extra[c * per + s], capacity) for s in range(per)]
+        known = jnp.concatenate(known, axis=1)
         weights_ref[...] = weight_rows(known)
 
         @pl.loop(0, feat_here // GROUP)
@@ -289,13 +331,16 @@
 
     for step in range(1, owners):
         send(step, step >= late_first).wait_send()
+        send_extra(step, step >= late_first).wait_send()
     for step in range(late_first, owners):
         send(step, True).wait_recv()
-
-
-def finish_kernel(late_ref, extra_ref, acc_ref, node_out, child_out, leaf_out):
-    sources = late_ref.shape[0]
-    extra = jnp.concatenate([extra_ref[s] for s in range(sources)], axis=1).astype(jnp.float32)
+        send_extra(step, True).wait_recv()
+
+
+def finish_kernel(late_ref, extra_ref, acc_ref, node_out, child_out, leaf_out, whole):
+    sources, group, capacity = late_ref.shape
+    extra = [unfold(extra_ref[s], capacity) for s in range(sources)]
+    extra = jnp.concatenate(extra, axis=1)
     bins = jnp.concatenate([late_ref[s] for s in range(sources)], axis=1).astype(jnp.float32)
     lane = lax.broadcasted_iota(jnp.int32, (16, 128), 1)
     for k, part in enumerate(pair_sums(bins, weight_rows(extra))):
@@ -309,17 +354,19 @@
                     full = jnp.where(lane < 64, parts[2 * t], turned[2 * t + 1])
                 else:
                     full = jnp.where(lane < 64, turned[2 * t], parts[2 * t + 1])
-                for q in range(4):
-                    for m in range(3):
-                        leaf_out[q, m, f : f + 1, 128 * t : 128 * t + 128] = full[
-                            3 * q + m : 3 * q + m + 1
-                        ]
-    for m in range(3):
-        a = leaf_out[0, m] + leaf_out[1, m]
-        b = leaf_out[2, m] + leaf_out[3, m]
-        child_out[0, m] = a
-        child_out[1, m] = b
-        node_out[0, m] = a + b
+                whole[t, 16 * f : 16 * f + 16] = full
+    for t in range(2):
+        lanes = slice(128 * t, 128 * t + 128)
+        for m in range(3):
+            leaves = []
+            for q in range(4):
+                leaf = whole[t, pl.ds(3 * q + m, group, stride=16)]
+                leaf_out[q, m, :, lanes] = leaf
+                leaves.append(leaf)
+            left, right = leaves[0] + leaves[1], leaves[2] + leaves[3]
+            child_out[0, m, :, lanes] = left
+            child_out[1, m, :, lanes] = right
+            node_out[0, m, :, lanes] = left + right
 
 
 def on_device(
@@ -337,22 +384,22 @@
 ):
     rows_here, feat_here = binned.shape
     node_count = root_feature.shape[0]
-    assert node_count == owners and owners >= 2 * AHEAD and owners & (owners - 1) == 0
+    assert node_count == owners and owners >= 2 * CHUNKS and owners & (owners - 1) == 0
     capacity = 2 * rows_here // node_count
     bf, f32, i32 = jnp.bfloat16, jnp.float32, jnp.int32
-    height = feat_here + EXTRA
     per = owners // CHUNKS
     dma = pltpu.SemaphoreType.DMA
     anywhere = pl.BlockSpec(memory_space=pltpu.HBM)
     vmem = pl.BlockSpec(memory_space=pltpu.VMEM)
-    late, acc = pl.pallas_call(
+    late, late_extra, acc = pl.pallas_call(
         functools.partial(exchange_kernel, owners, feat_devs, node_count, capacity),
         out_shape=(
-            jax.ShapeDtypeStruct((per, height, capacity), bf),
+            jax.ShapeDtypeStruct((per, feat_here, capacity), bf),
+            jax.ShapeDtypeStruct((per, EXTRA, LANES), bf),
             jax.ShapeDtypeStruct((feat_here // 2, 64, 128), f32),
         ),
         in_specs=[anywhere] * 9,
-        out_specs=(anywhere, vmem),
+        out_specs=(anywhere, anywhere, vmem),
         scratch_shapes=[
             pltpu.VMEM((feat_here, rows_here), i32),
             pltpu.VMEM((1, rows_here), i32),
@@ -365,15 +412,20 @@
             pltpu.VMEM((1, 2 * node_count), i32),
             pltpu.VMEM((16, rows_here // 4), bf),
             pltpu.VMEM((feat_devs - 1, 16, rows_here // 4), bf),
-            pltpu.VMEM((owners, height, capacity), bf),
-            pltpu.VMEM((owners - per, height, capacity), bf),
-            pltpu.VMEM((height, rows_here), bf),
+            pltpu.VMEM((owners, feat_here, capacity), bf),
+            pltpu.VMEM((owners, EXTRA, LANES), bf),
+            pltpu.VMEM((owners - per, feat_here, capacity), bf),
+            pltpu.VMEM((owners - per, EXTRA, LANES), bf),
+            pltpu.VMEM((feat_here, rows_here), bf),
+            pltpu.VMEM((EXTRA, rows_here), bf),
             pltpu.VMEM((1, rows_here), i32),
-            pltpu.VMEM((AHEAD, capacity, rows_here), bf),
+            pltpu.VMEM((owners // 2, capacity, rows_here), bf),
             pltpu.VMEM((16, per * capacity), bf),
             dma((9,)),
             dma((feat_devs - 1,)),
             dma((feat_devs - 1,)),
+            dma((owners,)),
+            dma((owners,)),
             dma((owners,)),
             dma((owners,)),
         ],
@@ -401,13 +453,14 @@
         ),
         in_specs=[
             pl.BlockSpec((per, GROUP, capacity), lambda i: (0, i, 0)),
-            pl.BlockSpec((per, EXTRA, capacity), lambda i: (0, feat_here // EXTRA, 0)),
+            pl.BlockSpec((per, EXTRA, LANES), lambda i: (0, 0, 0)),
             pl.BlockSpec((GROUP // 2, 64, 128), lambda i: (i, 0, 0)),
         ],
         out_specs=tuple(pl.BlockSpec((k, 3, GROUP, BINS), lambda i: (0, 0, i, 0)) for k in (1, 2, 4)),
+        scratch_shapes=[pltpu.VMEM((2, GROUP * 16, 128), f32)],
         compiler_params=pltpu.CompilerParams(vmem_limit_bytes=64 * 1024 * 1024),
         name="finish",
-    )(late, late, acc)
+    )(late, late_extra, acc)
 
 
 def solution(mesh):

time: 39.5 us -> 37.4 us (0.947)
  Pallas kernels: 38.6 us -> 36.5 us
    pallas_call x1, Pallas kernels: 32.9 us -> 30.9 us  [on_device(): pl.pallas_call(functools.partial(exchange_kernel, owners, feat_devs, node...]
where the time goes in v3:
time: 37.4 us; the launch traced here: 37.2 us
  Pallas kernels  36.5 us (98%)
  between operations  0.64 us (2%)
    pallas_call x1, Pallas kernels, on_device(): pl.pallas_call(functools.partial(exchange_kernel, owners, feat_devs, node...  30.9 us
    pallas_call x1, Pallas kernels, on_device(): pl.pallas_call(finish_kernel, grid=(feat_here // GROUP,), out_shape=tuple...  5.6 us

profile of v3, /device:TPU:0, one launch (start us, length us, event | category | flops | bytes accessed | tf_op | source)
XLA Modules:
  0.0 37.2 jit_solution(7016455592742300360)
XLA Ops:
  0.6 30.9 %exchange.1 = (bf16[2,64,512]{2,1,0:T(8,128)(2,1)}, bf16[2,16,128]{2,1,0:T(8,128)(2,1)}, f32[32,64,128]{2,1,0:T(8,128)}) custom-call(s32[64,2048]{1,0:T(8,128)} %bitcast.9, s32[1,2048]{1,0:T(1,128)} %bitcast.10, f32[1,2048]{1,0:T(1,128)} %bitcast.11, f32[1,2048]{1,0:T(1,128)} %bitcast.12, f32[1,2048]{1,0:T(1,128)} %bitcast.13, s32[1,8]{1,0:T(1,128)} %bitcast.14, ...), custom_call_target="tpu_custom_call" | custom-call | tf_op jit(solution)/shard_map/exchange/pallas_call | solution.py:394
  31.6 5.6 %finish.1 = (f32[1,3,64,256]{3,2,1,0:T(8,128)}, f32[2,3,64,256]{3,2,1,0:T(8,128)}, f32[4,3,64,256]{3,2,1,0:T(8,128)}) custom-call(bf16[2,64,512]{2,1,0:T(8,128)(2,1)} %get-tuple-element.6.late_ref, bf16[2,16,128]{2,1,0:T(8,128)(2,1)} %get-tuple-element.7.extra_ref, f32[32,64,128]{2,1,0:T(8,128)} %get-tuple-element.8.acc_ref), custom_call_target="tpu_custom_call" | custom-call | tf_op jit(solution)/shard_map/finish/pallas_call | solution.py:448

commit v4 on v3

--- a/solution.py
+++ b/solution.py
@@ -47,31 +47,28 @@
     return jnp.where(same, value, 0.0).astype(jnp.bfloat16)
 
 
-def pair_sums(bins, weights):
-    slots = bins.shape[1]
+def group_sums(high_ref, low_ref, group, weights):
+    slots = high_ref.shape[1]
     bf = jnp.bfloat16
-    high = jnp.floor(bins * (1.0 / 64.0))
-    low = (bins - 64.0 * high).astype(bf)
-    high = high.astype(bf)
     level = lax.broadcasted_iota(jnp.int32, (16, slots), 0).astype(jnp.float32).astype(bf)
     one, zero = jnp.ones((), bf), jnp.zeros((), bf)
+    left, right = [], []
+    for i in range(4):
+        row = pl.ds(4 * group + i, 1)
+        high = jnp.broadcast_to(high_ref[row], (16, slots)).astype(bf)
+        low = jnp.broadcast_to(low_ref[row], (16, slots)).astype(bf)
+        for c in range(4):
+            left.append(jnp.where(high == jnp.asarray(c, bf), weights, zero))
+            right.append(jnp.where(low == level + jnp.asarray(16 * c, bf), one, zero))
+    left = jnp.concatenate(left, axis=0)
+    right = jnp.concatenate(right, axis=0)
+    sums = lax.dot_general(left, right, NT, preferred_element_type=jnp.float32)
     lane = lax.broadcasted_iota(jnp.int32, (64, 128), 1)
     pairs = []
-    for base in range(0, GROUP, 4):
-        left, right = [], []
-        for f in range(base, base + 4):
-            high_f = jnp.broadcast_to(high[f : f + 1], (16, slots))
-            low_f = jnp.broadcast_to(low[f : f + 1], (16, slots))
-            for c in range(4):
-                left.append(jnp.where(high_f == jnp.asarray(c, bf), weights, zero))
-                right.append(jnp.where(low_f == level + jnp.asarray(16 * c, bf), one, zero))
-        left = jnp.concatenate(left, axis=0)
-        right = jnp.concatenate(right, axis=0)
-        sums = lax.dot_general(left, right, NT, preferred_element_type=jnp.float32)
-        for i in range(2):
-            even = sums[128 * i : 128 * i + 64, 128 * i : 128 * i + 128]
-            odd = sums[128 * i + 64 : 128 * i + 128, 128 * i : 128 * i + 128]
-            pairs.append(jnp.where(lane < 64, even, odd))
+    for i in range(2):
+        even = sums[128 * i : 128 * i + 64, 128 * i : 128 * i + 128]
+        odd = sums[128 * i + 64 : 128 * i + 128, 128 * i : 128 * i + 128]
+        pairs.append(jnp.where(lane < 64, even, odd))
     return pairs
 
 
@@ -89,8 +86,6 @@
     root_cut_hbm,
     child_feat_hbm,
     child_cut_hbm,
-    late_ref,
-    late_extra_ref,
     acc_ref,
     bins_in,
     node_in,
@@ -112,6 +107,8 @@
     slot_ref,
     places,
     weights_ref,
+    high_ref,
+    low_ref,
     in_sem,
     pick_send_sem,
     pick_recv_sem,
@@ -226,55 +223,53 @@
 
     half = owners // 2
     per = owners // CHUNKS
-    late_first = owners - per
     block = min(256, capacity)
     level = lax.broadcasted_iota(jnp.int32, (16, rows_here), 0).astype(jnp.float32).astype(bf)
     one, zero = jnp.ones((), bf), jnp.zeros((), bf)
 
     def fill(step, where):
         target = slot_ref[...] - partner_of(me, step, owners) * capacity
-        for start in range(0, capacity, block):
-            inside = target - start
+
+        @pl.loop(0, capacity // block)
+        def _(part):
+            inside = target - part * block
             inside = jnp.where((inside >= 0) & (inside < block), inside, -1)
             inside = inside.astype(jnp.float32).astype(bf)
             inside = jnp.broadcast_to(inside, (16, rows_here))
             for k in range(0, block, 16):
-                places[where, start + k : start + k + 16] = jnp.where(
-                    inside == level + jnp.asarray(k, bf), one, zero
-                )
+                rows = pl.ds(pl.multiple_of(part * block + k, 16), 16)
+                places[where, rows] = jnp.where(inside == level + jnp.asarray(k, bf), one, zero)
 
     def moved(rows_ref, where):
         return lax.dot_general(
             rows_ref[...], places[where], NT, preferred_element_type=jnp.float32
         )
 
-    def send(step, late):
+    def send(step):
         return pltpu.make_async_remote_copy(
             src_ref=blocks.at[step],
-            dst_ref=late_ref.at[step - late_first] if late else got.at[step],
+            dst_ref=got.at[step],
             send_sem=send_sem.at[step],
             recv_sem=recv_sem.at[step],
             device_id={"rows": partner_of(me, step, owners)},
             device_id_type=MESH,
         )
 
-    def send_extra(step, late):
+    def send_extra(step):
         return pltpu.make_async_remote_copy(
             src_ref=extra_blocks.at[step],
-            dst_ref=late_extra_ref.at[step - late_first] if late else got_extra.at[step],
+            dst_ref=got_extra.at[step],
             send_sem=extra_send_sem.at[step],
             recv_sem=extra_recv_sem.at[step],
             device_id={"rows": partner_of(me, step, owners)},
             device_id_type=MESH,
         )
 
-    for start, stop, late in ((half, late_first, False), (late_first, owners, True)):
-
-        @pl.loop(start, stop)
-        def _(step):
-            fill(step, step - half)
-            blocks[step] = moved(bins_rows, step - half).astype(bf)
-            send(step, late).start()
+    @pl.loop(half, owners)
+    def _(step):
+        fill(step, step - half)
+        blocks[step] = moved(bins_rows, step - half).astype(bf)
+        send(step).start()
 
     weight, treat, result = weight_in[...], treat_in[...], result_in[...]
     scaled = weight * treat
@@ -292,59 +287,58 @@
     extra = jnp.concatenate([weight, scaled * treat, scaled * result, leaf, none], axis=0)
     extra_rows[...] = extra.astype(bf)
 
-    for start, stop, late in ((half, late_first, False), (late_first, owners, True)):
-
-        @pl.loop(start, stop)
-        def _(step):
-            extra_blocks[step] = fold(moved(extra_rows, step - half)).astype(bf)
-            send_extra(step, late).start()
-
-    @pl.loop(1, half)
+    @pl.loop(0, half)
     def _(back):
-        step = half - back
-        fill(step, step)
-        blocks[step] = moved(bins_rows, step).astype(bf)
-        send(step, False).start()
-        extra_blocks[step] = fold(moved(extra_rows, step)).astype(bf)
-        send_extra(step, False).start()
-
-    fill(0, 0)
-    got[0] = moved(bins_rows, 0).astype(bf)
-    got_extra[0] = fold(moved(extra_rows, 0)).astype(bf)
-
-    for c in range(CHUNKS - 1):
-        for step in range(max(1, c * per), (c + 1) * per):
-            send(step, False).wait_recv()
-            send_extra(step, False).wait_recv()
+        far, near = owners - 1 - back, half - 1 - back
+        extra_blocks[far] = fold(moved(extra_rows, near)).astype(bf)
+        send_extra(far).start()
+        fill(near, near)
+        blocks[near] = moved(bins_rows, near).astype(bf)
+        extra_blocks[near] = fold(moved(extra_rows, near)).astype(bf)
+
+        @pl.when(near > 0)
+        def _():
+            send(near).start()
+            send_extra(near).start()
+
+    got[0] = blocks[0]
+    got_extra[0] = extra_blocks[0]
+    acc_ref[...] = jnp.zeros_like(acc_ref)
+
+    @pl.loop(0, CHUNKS)
+    def _(c):
+        for s in range(per):
+            step = c * per + s
+
+            @pl.when(step > 0)
+            def _():
+                send(step).wait_recv()
+                send_extra(step).wait_recv()
+
         known = [unfold(got_extra[c * per + s], capacity) for s in range(per)]
-        known = jnp.concatenate(known, axis=1)
-        weights_ref[...] = weight_rows(known)
-
-        @pl.loop(0, feat_here // GROUP)
-        def _(block):
-            rows = pl.ds(pl.multiple_of(block * GROUP, GROUP), GROUP)
-            values = jnp.concatenate([got[c * per + s, rows] for s in range(per)], axis=1)
-            sums = pair_sums(values.astype(jnp.float32), weights_ref[...])
-            for k, part in enumerate(sums):
-                spot = block * (GROUP // 2) + k
-                acc_ref[spot] = part if c == 0 else acc_ref[spot] + part
-
-    for step in range(1, owners):
-        send(step, step >= late_first).wait_send()
-        send_extra(step, step >= late_first).wait_send()
-    for step in range(late_first, owners):
-        send(step, True).wait_recv()
-        send_extra(step, True).wait_recv()
-
-
-def finish_kernel(late_ref, extra_ref, acc_ref, node_out, child_out, leaf_out, whole):
-    sources, group, capacity = late_ref.shape
-    extra = [unfold(extra_ref[s], capacity) for s in range(sources)]
-    extra = jnp.concatenate(extra, axis=1)
-    bins = jnp.concatenate([late_ref[s] for s in range(sources)], axis=1).astype(jnp.float32)
+        weights_ref[...] = weight_rows(jnp.concatenate(known, axis=1))
+        for s in range(per):
+            bins = got[c * per + s].astype(jnp.float32)
+            high = jnp.floor(bins * (1.0 / 64.0))
+            high_ref[:, s * capacity : (s + 1) * capacity] = high
+            low_ref[:, s * capacity : (s + 1) * capacity] = bins - 64.0 * high
+
+        @pl.loop(0, feat_here // 4)
+        def _(group):
+            for k, part in enumerate(group_sums(high_ref, low_ref, group, weights_ref[...])):
+                acc_ref[2 * group + k] += part
+
+    @pl.loop(1, owners)
+    def _(step):
+        send(step).wait_send()
+        send_extra(step).wait_send()
+
+
+def finish_kernel(acc_ref, node_out, child_out, leaf_out, whole):
     lane = lax.broadcasted_iota(jnp.int32, (16, 128), 1)
-    for k, part in enumerate(pair_sums(bins, weight_rows(extra))):
-        part = part + acc_ref[k]
+    group = 2 * acc_ref.shape[0]
+    for k in range(group // 2):
+        part = acc_ref[k]
         parts = [part[16 * c : 16 * c + 16] for c in range(4)]
         turned = [pltpu.roll(p, 64, 1) for p in parts]
         for i in range(2):
@@ -391,15 +385,11 @@
     dma = pltpu.SemaphoreType.DMA
     anywhere = pl.BlockSpec(memory_space=pltpu.HBM)
     vmem = pl.BlockSpec(memory_space=pltpu.VMEM)
-    late, late_extra, acc = pl.pallas_call(
+    acc = pl.pallas_call(
         functools.partial(exchange_kernel, owners, feat_devs, node_count, capacity),
-        out_shape=(
-            jax.ShapeDtypeStruct((per, feat_here, capacity), bf),
-            jax.ShapeDtypeStruct((per, EXTRA, LANES), bf),
-            jax.ShapeDtypeStruct((feat_here // 2, 64, 128), f32),
-        ),
+        out_shape=jax.ShapeDtypeStruct((feat_here // 2, 64, 128), f32),
         in_specs=[anywhere] * 9,
-        out_specs=(anywhere, anywhere, vmem),
+        out_specs=vmem,
         scratch_shapes=[
             pltpu.VMEM((feat_here, rows_here), i32),
             pltpu.VMEM((1, rows_here), i32),
@@ -414,13 +404,15 @@
             pltpu.VMEM((feat_devs - 1, 16, rows_here // 4), bf),
             pltpu.VMEM((owners, feat_here, capacity), bf),
             pltpu.VMEM((owners, EXTRA, LANES), bf),
-            pltpu.VMEM((owners - per, feat_here, capacity), bf),
-            pltpu.VMEM((owners - per, EXTRA, LANES), bf),
+            pltpu.VMEM((owners, feat_here, capacity), bf),
+            pltpu.VMEM((owners, EXTRA, LANES), bf),
             pltpu.VMEM((feat_here, rows_here), bf),
             pltpu.VMEM((EXTRA, rows_here), bf),
             pltpu.VMEM((1, rows_here), i32),
             pltpu.VMEM((owners // 2, capacity, rows_here), bf),
             pltpu.VMEM((16, per * capacity), bf),
+            pltpu.VMEM((feat_here, per * capacity), f32),
+            pltpu.VMEM((feat_here, per * capacity), f32),
             dma((9,)),
             dma((feat_devs - 1,)),
             dma((feat_devs - 1,)),
@@ -452,15 +444,13 @@
             jax.ShapeDtypeStruct((k, 3, feat_here, BINS), f32) for k in (1, 2, 4)
         ),
         in_specs=[
-            pl.BlockSpec((per, GROUP, capacity), lambda i: (0, i, 0)),
-            pl.BlockSpec((per, EXTRA, LANES), lambda i: (0, 0, 0)),
             pl.BlockSpec((GROUP // 2, 64, 128), lambda i: (i, 0, 0)),
         ],
         out_specs=tuple(pl.BlockSpec((k, 3, GROUP, BINS), lambda i: (0, 0, i, 0)) for k in (1, 2, 4)),
         scratch_shapes=[pltpu.VMEM((2, GROUP * 16, 128), f32)],
         compiler_params=pltpu.CompilerParams(vmem_limit_bytes=64 * 1024 * 1024),
         name="finish",
-    )(late, late_extra, acc)
+    )(acc)
 
 
 def solution(mesh):

time: 37.4 us -> 49 us (1.31)
  Pallas kernels: 36.5 us -> 48.1 us
    pallas_call x1, Pallas kernels: 30.9 us -> 44.3 us  [on_device(): pl.pallas_call(functools.partial(exchange_kernel, owners, feat_devs, node...]
    pallas_call x1, Pallas kernels: 5.6 us -> 3.75 us  [on_device(): pl.pallas_call(finish_kernel, grid=(feat_here // GROUP,), out_shape=tuple...]
where the time goes in v4:
time: 49 us; the launch traced here: 48.7 us
  Pallas kernels  48.1 us (98%)
  between operations  0.64 us (1%)
    pallas_call x1, Pallas kernels, on_device(): pl.pallas_call(functools.partial(exchange_kernel, owners, feat_devs, node...  44.3 us
    pallas_call x1, Pallas kernels, on_device(): pl.pallas_call(finish_kernel, grid=(feat_here // GROUP,), out_shape=tuple...  3.75 us

profile of v4, /device:TPU:0, one launch (start us, length us, event | category | flops | bytes accessed | tf_op | source)
XLA Modules:
  0.0 48.7 jit_solution(16193470934292091473)
XLA Ops:
  0.6 44.3 %exchange.1.acc_ref = f32[32,64,128]{2,1,0:T(8,128)} custom-call(s32[64,2048]{1,0:T(8,128)} %bitcast.9, s32[1,2048]{1,0:T(1,128)} %bitcast.10, f32[1,2048]{1,0:T(1,128)} %bitcast.11, f32[1,2048]{1,0:T(1,128)} %bitcast.12, f32[1,2048]{1,0:T(1,128)} %bitcast.13, s32[1,8]{1,0:T(1,128)} %bitcast.14, s32[1,8]{1,0:T(1,128)} %bitcast.15, s32[1,16]{1,0:T(1,128)} %bitcast.16, ...), custom_call_target="tpu_custom_call" | custom-call | tf_op jit(solution)/shard_map/exchange/pallas_call | solution.py:388
  45.0 3.8 %finish.1 = (f32[1,3,64,256]{3,2,1,0:T(8,128)}, f32[2,3,64,256]{3,2,1,0:T(8,128)}, f32[4,3,64,256]{3,2,1,0:T(8,128)}) custom-call(f32[32,64,128]{2,1,0:T(8,128)} %exchange.1.acc_ref), custom_call_target="tpu_custom_call" | custom-call | tf_op jit(solution)/shard_map/finish/pallas_call | solution.py:440

commit v5 on v4

--- a/solution.py
+++ b/solution.py
@@ -47,28 +47,31 @@
     return jnp.where(same, value, 0.0).astype(jnp.bfloat16)
 
 
-def group_sums(high_ref, low_ref, group, weights):
-    slots = high_ref.shape[1]
+def pair_sums(bins, weights):
+    slots = bins.shape[1]
     bf = jnp.bfloat16
+    high = jnp.floor(bins * (1.0 / 64.0))
+    low = (bins - 64.0 * high).astype(bf)
+    high = high.astype(bf)
     level = lax.broadcasted_iota(jnp.int32, (16, slots), 0).astype(jnp.float32).astype(bf)
     one, zero = jnp.ones((), bf), jnp.zeros((), bf)
-    left, right = [], []
-    for i in range(4):
-        row = pl.ds(4 * group + i, 1)
-        high = jnp.broadcast_to(high_ref[row], (16, slots)).astype(bf)
-        low = jnp.broadcast_to(low_ref[row], (16, slots)).astype(bf)
-        for c in range(4):
-            left.append(jnp.where(high == jnp.asarray(c, bf), weights, zero))
-            right.append(jnp.where(low == level + jnp.asarray(16 * c, bf), one, zero))
-    left = jnp.concatenate(left, axis=0)
-    right = jnp.concatenate(right, axis=0)
-    sums = lax.dot_general(left, right, NT, preferred_element_type=jnp.float32)
     lane = lax.broadcasted_iota(jnp.int32, (64, 128), 1)
     pairs = []
-    for i in range(2):
-        even = sums[128 * i : 128 * i + 64, 128 * i : 128 * i + 128]
-        odd = sums[128 * i + 64 : 128 * i + 128, 128 * i : 128 * i + 128]
-        pairs.append(jnp.where(lane < 64, even, odd))
+    for base in range(0, GROUP, 4):
+        left, right = [], []
+        for f in range(base, base + 4):
+            high_f = jnp.broadcast_to(high[f : f + 1], (16, slots))
+            low_f = jnp.broadcast_to(low[f : f + 1], (16, slots))
+            for c in range(4):
+                left.append(jnp.where(high_f == jnp.asarray(c, bf), weights, zero))
+                right.append(jnp.where(low_f == level + jnp.asarray(16 * c, bf), one, zero))
+        left = jnp.concatenate(left, axis=0)
+        right = jnp.concatenate(right, axis=0)
+        sums = lax.dot_general(left, right, NT, preferred_element_type=jnp.float32)
+        for i in range(2):
+            even = sums[128 * i : 128 * i + 64, 128 * i : 128 * i + 128]
+            odd = sums[128 * i + 64 : 128 * i + 128, 128 * i : 128 * i + 128]
+            pairs.append(jnp.where(lane < 64, even, odd))
     return pairs
 
 
@@ -102,13 +105,10 @@
     extra_blocks,
     got,
     got_extra,
-    bins_rows,
-    extra_rows,
+    rows_in,
     slot_ref,
     places,
     weights_ref,
-    high_ref,
-    low_ref,
     in_sem,
     pick_send_sem,
     pick_recv_sem,
@@ -154,7 +154,7 @@
         load.wait()
     node = node_in[...]
     bins = bins_in[...].astype(jnp.float32).astype(bf)
-    bins_rows[...] = bins
+    rows_in[0:feat_here] = bins
     chosen = lax.broadcasted_iota(jnp.int32, (node_count, rows_here), 0) == node
 
     def column(table, stride, first):
@@ -240,10 +240,10 @@
                 rows = pl.ds(pl.multiple_of(part * block + k, 16), 16)
                 places[where, rows] = jnp.where(inside == level + jnp.asarray(k, bf), one, zero)
 
-    def moved(rows_ref, where):
-        return lax.dot_general(
-            rows_ref[...], places[where], NT, preferred_element_type=jnp.float32
-        )
+    def pack(step, where):
+        moved = lax.dot_general(rows_in[...], places[where], NT, preferred_element_type=jnp.float32)
+        blocks[step] = moved[0:feat_here].astype(bf)
+        extra_blocks[step] = fold(moved[feat_here : feat_here + EXTRA]).astype(bf)
 
     def send(step):
         return pltpu.make_async_remote_copy(
@@ -268,8 +268,6 @@
     @pl.loop(half, owners)
     def _(step):
         fill(step, step - half)
-        blocks[step] = moved(bins_rows, step - half).astype(bf)
-        send(step).start()
 
     weight, treat, result = weight_in[...], treat_in[...], result_in[...]
     scaled = weight * treat
@@ -285,21 +283,24 @@
     leaf = jnp.where(right_root, 2.0 + second, first)
     none = jnp.zeros((EXTRA - 4, rows_here), jnp.float32)
     extra = jnp.concatenate([weight, scaled * treat, scaled * result, leaf, none], axis=0)
-    extra_rows[...] = extra.astype(bf)
+    rows_in[feat_here : feat_here + EXTRA] = extra.astype(bf)
+
+    @pl.loop(half, owners)
+    def _(step):
+        pack(step, step - half)
+        send(step).start()
+        send_extra(step).start()
 
     @pl.loop(0, half)
     def _(back):
-        far, near = owners - 1 - back, half - 1 - back
-        extra_blocks[far] = fold(moved(extra_rows, near)).astype(bf)
-        send_extra(far).start()
-        fill(near, near)
-        blocks[near] = moved(bins_rows, near).astype(bf)
-        extra_blocks[near] = fold(moved(extra_rows, near)).astype(bf)
-
-        @pl.when(near > 0)
+        step = half - 1 - back
+        fill(step, step)
+        pack(step, step)
+
+        @pl.when(step > 0)
         def _():
-            send(near).start()
-            send_extra(near).start()
+            send(step).start()
+            send_extra(step).start()
 
     got[0] = blocks[0]
     got_extra[0] = extra_blocks[0]
@@ -317,16 +318,13 @@
 
         known = [unfold(got_extra[c * per + s], capacity) for s in range(per)]
         weights_ref[...] = weight_rows(jnp.concatenate(known, axis=1))
-        for s in range(per):
-            bins = got[c * per + s].astype(jnp.float32)
-            high = jnp.floor(bins * (1.0 / 64.0))
-            high_ref[:, s * capacity : (s + 1) * capacity] = high
-            low_ref[:, s * capacity : (s + 1) * capacity] = bins - 64.0 * high
-
-        @pl.loop(0, feat_here // 4)
-        def _(group):
-            for k, part in enumerate(group_sums(high_ref, low_ref, group, weights_ref[...])):
-                acc_ref[2 * group + k] += part
+
+        @pl.loop(0, feat_here // GROUP)
+        def _(part):
+            rows = pl.ds(pl.multiple_of(part * GROUP, GROUP), GROUP)
+            values = jnp.concatenate([got[c * per + s, rows] for s in range(per)], axis=1)
+            for k, sums in enumerate(pair_sums(values.astype(jnp.float32), weights_ref[...])):
+                acc_ref[part * (GROUP // 2) + k] += sums
 
     @pl.loop(1, owners)
     def _(step):
@@ -406,13 +404,10 @@
             pltpu.VMEM((owners, EXTRA, LANES), bf),
             pltpu.VMEM((owners, feat_here, capacity), bf),
             pltpu.VMEM((owners, EXTRA, LANES), bf),
-            pltpu.VMEM((feat_here, rows_here), bf),
-            pltpu.VMEM((EXTRA, rows_here), bf),
+            pltpu.VMEM((feat_here + EXTRA, rows_here), bf),
             pltpu.VMEM((1, rows_here), i32),
             pltpu.VMEM((owners // 2, capacity, rows_here), bf),
             pltpu.VMEM((16, per * capacity), bf),
-            pltpu.VMEM((feat_here, per * capacity), f32),
-            pltpu.VMEM((feat_here, per * capacity), f32),
             dma((9,)),
             dma((feat_devs - 1,)),
             dma((feat_devs - 1,)),

time: 49 us -> 40.7 us (0.83)
  Pallas kernels: 48.1 us -> 39.8 us
    pallas_call x1, Pallas kernels: 44.3 us -> 36.1 us  [on_device(): pl.pallas_call(functools.partial(exchange_kernel, owners, feat_devs, node...]
where the time goes in v5:
time: 40.7 us; the launch traced here: 40.5 us
  Pallas kernels  39.8 us (98%)
  between operations  0.64 us (2%)
    pallas_call x1, Pallas kernels, on_device(): pl.pallas_call(functools.partial(exchange_kernel, owners, feat_devs, node...  36.1 us
    pallas_call x1, Pallas kernels, on_device(): pl.pallas_call(finish_kernel, grid=(feat_here // GROUP,), out_shape=tuple...  3.75 us

profile of v5, /device:TPU:0, one launch (start us, length us, event | category | flops | bytes accessed | tf_op | source)
XLA Modules:
  0.0 40.5 jit_solution(5830039104277610558)
XLA Ops:
  0.6 36.1 %exchange.1.acc_ref = f32[32,64,128]{2,1,0:T(8,128)} custom-call(s32[64,2048]{1,0:T(8,128)} %bitcast.9, s32[1,2048]{1,0:T(1,128)} %bitcast.10, f32[1,2048]{1,0:T(1,128)} %bitcast.11, f32[1,2048]{1,0:T(1,128)} %bitcast.12, f32[1,2048]{1,0:T(1,128)} %bitcast.13, s32[1,8]{1,0:T(1,128)} %bitcast.14, s32[1,8]{1,0:T(1,128)} %bitcast.15, s32[1,16]{1,0:T(1,128)} %bitcast.16, ...), custom_call_target="tpu_custom_call" | custom-call | tf_op jit(solution)/shard_map/exchange/pallas_call | solution.py:386
  36.7 3.8 %finish.1 = (f32[1,3,64,256]{3,2,1,0:T(8,128)}, f32[2,3,64,256]{3,2,1,0:T(8,128)}, f32[4,3,64,256]{3,2,1,0:T(8,128)}) custom-call(f32[32,64,128]{2,1,0:T(8,128)} %exchange.1.acc_ref), custom_call_target="tpu_custom_call" | custom-call | tf_op jit(solution)/shard_map/finish/pallas_call | solution.py:435

commit v6 on v5

--- a/solution.py
+++ b/solution.py
@@ -150,12 +150,86 @@
             barrier, inc=1, device_id={"feat": lax.rem(mine + step, feat_devs)}, device_id_type=MESH
         )
 
-    for load in loads:
+    for load in loads[:2]:
         load.wait()
     node = node_in[...]
     bins = bins_in[...].astype(jnp.float32).astype(bf)
     rows_in[0:feat_here] = bins
     chosen = lax.broadcasted_iota(jnp.int32, (node_count, rows_here), 0) == node
+
+    chunk = 256
+    ones = chosen.astype(jnp.float32)
+    up_to = lax.broadcasted_iota(jnp.int32, (chunk, chunk), 0) <= lax.broadcasted_iota(
+        jnp.int32, (chunk, chunk), 1
+    )
+    up_to = up_to.astype(jnp.float32).astype(bf)
+    before = jnp.zeros((node_count, 1), jnp.float32)
+    ranks = []
+    for k in range(rows_here // chunk):
+        here = ones[:, k * chunk : (k + 1) * chunk]
+        counts = jnp.dot(here.astype(bf), up_to, preferred_element_type=jnp.float32) + before
+        ranks.append(jnp.sum(here * counts, axis=0, keepdims=True))
+        before = before + jnp.sum(here, axis=1, keepdims=True)
+    rank = jnp.concatenate(ranks, axis=1).astype(jnp.int32) - 1
+    slot_ref[...] = node * capacity + rank
+
+    half = owners // 2
+    per = owners // CHUNKS
+    block = min(256, capacity)
+    level = lax.broadcasted_iota(jnp.int32, (16, rows_here), 0).astype(jnp.float32).astype(bf)
+    one, zero = jnp.ones((), bf), jnp.zeros((), bf)
+
+    def fill(step, where):
+        target = slot_ref[...] - partner_of(me, step, owners) * capacity
+
+        @pl.loop(0, capacity // block)
+        def _(part):
+            inside = target - part * block
+            inside = jnp.where((inside >= 0) & (inside < block), inside, -1)
+            inside = inside.astype(jnp.float32).astype(bf)
+            inside = jnp.broadcast_to(inside, (16, rows_here))
+            for k in range(0, block, 16):
+                rows = pl.ds(pl.multiple_of(part * block + k, 16), 16)
+                places[where, rows] = jnp.where(inside == level + jnp.asarray(k, bf), one, zero)
+
+    def pack(step, where):
+        moved = lax.dot_general(rows_in[...], places[where], NT, preferred_element_type=jnp.float32)
+        blocks[step] = moved[0:feat_here].astype(bf)
+        extra_blocks[step] = fold(moved[feat_here : feat_here + EXTRA]).astype(bf)
+
+    def send(step):
+        return pltpu.make_async_remote_copy(
+            src_ref=blocks.at[step],
+            dst_ref=got.at[step],
+            send_sem=send_sem.at[step],
+            recv_sem=recv_sem.at[step],
+            device_id={"rows": partner_of(me, step, owners)},
+            device_id_type=MESH,
+        )
+
+    def send_extra(step):
+        return pltpu.make_async_remote_copy(
+            src_ref=extra_blocks.at[step],
+            dst_ref=got_extra.at[step],
+            send_sem=extra_send_sem.at[step],
+            recv_sem=extra_recv_sem.at[step],
+            device_id={"rows": partner_of(me, step, owners)},
+            device_id_type=MESH,
+        )
+
+    def far(step):
+        fill(step, step - half)
+        moved = lax.dot_general(
+            rows_in[0:feat_here], places[step - half], NT, preferred_element_type=jnp.float32
+        )
+        blocks[step] = moved.astype(bf)
+        send(step).start()
+
+    pl.semaphore_wait(barrier, owners - 1 + feat_devs - 1)
+    far(half)
+
+    for load in loads[2:]:
+        load.wait()
 
     def column(table, stride, first):
         width = table.shape[1]
@@ -190,8 +264,6 @@
     folded = jnp.concatenate([picks[:, k * quarter : (k + 1) * quarter] for k in range(4)], axis=0)
     pick_send[...] = folded.astype(bf)
 
-    pl.semaphore_wait(barrier, owners - 1 + feat_devs - 1)
-
     pick_copies = []
     for step in range(1, feat_devs):
         copy = pltpu.make_async_remote_copy(
@@ -205,69 +277,9 @@
         copy.start()
         pick_copies.append(copy)
 
-    chunk = 256
-    ones = chosen.astype(jnp.float32)
-    up_to = lax.broadcasted_iota(jnp.int32, (chunk, chunk), 0) <= lax.broadcasted_iota(
-        jnp.int32, (chunk, chunk), 1
-    )
-    up_to = up_to.astype(jnp.float32).astype(bf)
-    before = jnp.zeros((node_count, 1), jnp.float32)
-    ranks = []
-    for k in range(rows_here // chunk):
-        here = ones[:, k * chunk : (k + 1) * chunk]
-        counts = jnp.dot(here.astype(bf), up_to, preferred_element_type=jnp.float32) + before
-        ranks.append(jnp.sum(here * counts, axis=0, keepdims=True))
-        before = before + jnp.sum(here, axis=1, keepdims=True)
-    rank = jnp.concatenate(ranks, axis=1).astype(jnp.int32) - 1
-    slot_ref[...] = node * capacity + rank
-
-    half = owners // 2
-    per = owners // CHUNKS
-    block = min(256, capacity)
-    level = lax.broadcasted_iota(jnp.int32, (16, rows_here), 0).astype(jnp.float32).astype(bf)
-    one, zero = jnp.ones((), bf), jnp.zeros((), bf)
-
-    def fill(step, where):
-        target = slot_ref[...] - partner_of(me, step, owners) * capacity
-
-        @pl.loop(0, capacity // block)
-        def _(part):
-            inside = target - part * block
-            inside = jnp.where((inside >= 0) & (inside < block), inside, -1)
-            inside = inside.astype(jnp.float32).astype(bf)
-            inside = jnp.broadcast_to(inside, (16, rows_here))
-            for k in range(0, block, 16):
-                rows = pl.ds(pl.multiple_of(part * block + k, 16), 16)
-                places[where, rows] = jnp.where(inside == level + jnp.asarray(k, bf), one, zero)
-
-    def pack(step, where):
-        moved = lax.dot_general(rows_in[...], places[where], NT, preferred_element_type=jnp.float32)
-        blocks[step] = moved[0:feat_here].astype(bf)
-        extra_blocks[step] = fold(moved[feat_here : feat_here + EXTRA]).astype(bf)
-
-    def send(step):
-        return pltpu.make_async_remote_copy(
-            src_ref=blocks.at[step],
-            dst_ref=got.at[step],
-            send_sem=send_sem.at[step],
-            recv_sem=recv_sem.at[step],
-            device_id={"rows": partner_of(me, step, owners)},
-            device_id_type=MESH,
-        )
-
-    def send_extra(step):
-        return pltpu.make_async_remote_copy(
-            src_ref=extra_blocks.at[step],
-            dst_ref=got_extra.at[step],
-            send_sem=extra_send_sem.at[step],
-            recv_sem=extra_recv_sem.at[step],
-            device_id={"rows": partner_of(me, step, owners)},
-            device_id_type=MESH,
-        )
-
-    @pl.loop(half, owners)
+    @pl.loop(half + 1, owners)
     def _(step):
-        fill(step, step - half)
+        far(step)
 
     weight, treat, result = weight_in[...], treat_in[...], result_in[...]
     scaled = weight * treat
@@ -287,8 +299,13 @@
 
     @pl.loop(half, owners)
     def _(step):
-        pack(step, step - half)
-        send(step).start()
+        moved = lax.dot_general(
+            rows_in[feat_here : feat_here + EXTRA],
+            places[step - half],
+            NT,
+            preferred_element_type=jnp.float32,
+        )
+        extra_blocks[step] = fold(moved).astype(bf)
         send_extra(step).start()
 
     @pl.loop(0, half)

time: 40.7 us -> 38.9 us (0.956)
  Pallas kernels: 39.8 us -> 38 us
    pallas_call x1, Pallas kernels: 36.1 us -> 34.3 us  [on_device(): pl.pallas_call(functools.partial(exchange_kernel, owners, feat_devs, node...]
where the time goes in v6:
time: 38.9 us; the launch traced here: 38.7 us
  Pallas kernels  38 us (98%)
  between operations  0.64 us (2%)
    pallas_call x1, Pallas kernels, on_device(): pl.pallas_call(functools.partial(exchange_kernel, owners, feat_devs, node...  34.3 us
    pallas_call x1, Pallas kernels, on_device(): pl.pallas_call(finish_kernel, grid=(feat_here // GROUP,), out_shape=tuple...  3.75 us

profile of v6, /device:TPU:0, one launch (start us, length us, event | category | flops | bytes accessed | tf_op | source)
XLA Modules:
  0.0 38.7 jit_solution(13016999034378380336)
XLA Ops:
  0.6 34.3 %exchange.1.acc_ref = f32[32,64,128]{2,1,0:T(8,128)} custom-call(s32[64,2048]{1,0:T(8,128)} %bitcast.9, s32[1,2048]{1,0:T(1,128)} %bitcast.10, f32[1,2048]{1,0:T(1,128)} %bitcast.11, f32[1,2048]{1,0:T(1,128)} %bitcast.12, f32[1,2048]{1,0:T(1,128)} %bitcast.13, s32[1,8]{1,0:T(1,128)} %bitcast.14, s32[1,8]{1,0:T(1,128)} %bitcast.15, s32[1,16]{1,0:T(1,128)} %bitcast.16, ...), custom_call_target="tpu_custom_call" | custom-call | tf_op jit(solution)/shard_map/exchange/pallas_call | solution.py:403
  34.9 3.8 %finish.1 = (f32[1,3,64,256]{3,2,1,0:T(8,128)}, f32[2,3,64,256]{3,2,1,0:T(8,128)}, f32[4,3,64,256]{3,2,1,0:T(8,128)}) custom-call(f32[32,64,128]{2,1,0:T(8,128)} %exchange.1.acc_ref), custom_call_target="tpu_custom_call" | custom-call | tf_op jit(solution)/shard_map/finish/pallas_call | solution.py:452

commit v7 on v3

--- a/solution.py
+++ b/solution.py
@@ -107,8 +107,7 @@
     extra_blocks,
     got,
     got_extra,
-    bins_rows,
-    extra_rows,
+    rows_in,
     slot_ref,
     places,
     weights_ref,
@@ -157,7 +156,7 @@
         load.wait()
     node = node_in[...]
     bins = bins_in[...].astype(jnp.float32).astype(bf)
-    bins_rows[...] = bins
+    rows_in[0:feat_here] = bins
     chosen = lax.broadcasted_iota(jnp.int32, (node_count, rows_here), 0) == node
 
     def column(table, stride, first):
@@ -243,9 +242,9 @@
                     inside == level + jnp.asarray(k, bf), one, zero
                 )
 
-    def moved(rows_ref, where):
+    def moved(first, last, where):
         return lax.dot_general(
-            rows_ref[...], places[where], NT, preferred_element_type=jnp.float32
+            rows_in[first:last], places[where], NT, preferred_element_type=jnp.float32
         )
 
     def send(step, late):
@@ -273,7 +272,7 @@
         @pl.loop(start, stop)
         def _(step):
             fill(step, step - half)
-            blocks[step] = moved(bins_rows, step - half).astype(bf)
+            blocks[step] = moved(0, feat_here, step - half).astype(bf)
             send(step, late).start()
 
     weight, treat, result = weight_in[...], treat_in[...], result_in[...]
@@ -290,27 +289,30 @@
     leaf = jnp.where(right_root, 2.0 + second, first)
     none = jnp.zeros((EXTRA - 4, rows_here), jnp.float32)
     extra = jnp.concatenate([weight, scaled * treat, scaled * result, leaf, none], axis=0)
-    extra_rows[...] = extra.astype(bf)
+    rows_in[feat_here : feat_here + EXTRA] = extra.astype(bf)
 
     for start, stop, late in ((half, late_first, False), (late_first, owners, True)):
 
         @pl.loop(start, stop)
         def _(step):
-            extra_blocks[step] = fold(moved(extra_rows, step - half)).astype(bf)
+            tail = moved(feat_here, feat_here + EXTRA, step - half)
+            extra_blocks[step] = fold(tail).astype(bf)
             send_extra(step, late).start()
 
     @pl.loop(1, half)
     def _(back):
         step = half - back
         fill(step, step)
-        blocks[step] = moved(bins_rows, step).astype(bf)
+        both = moved(0, feat_here + EXTRA, step)
+        blocks[step] = both[0:feat_here].astype(bf)
+        extra_blocks[step] = fold(both[feat_here : feat_here + EXTRA]).astype(bf)
         send(step, False).start()
-        extra_blocks[step] = fold(moved(extra_rows, step)).astype(bf)
         send_extra(step, False).start()
 
     fill(0, 0)
-    got[0] = moved(bins_rows, 0).astype(bf)
-    got_extra[0] = fold(moved(extra_rows, 0)).astype(bf)
+    both = moved(0, feat_here + EXTRA, 0)
+    got[0] = both[0:feat_here].astype(bf)
+    got_extra[0] = fold(both[feat_here : feat_here + EXTRA]).astype(bf)
 
     for c in range(CHUNKS - 1):
         for step in range(max(1, c * per), (c + 1) * per):
@@ -416,8 +418,7 @@
             pltpu.VMEM((owners, EXTRA, LANES), bf),
             pltpu.VMEM((owners - per, feat_here, capacity), bf),
             pltpu.VMEM((owners - per, EXTRA, LANES), bf),
-            pltpu.VMEM((feat_here, rows_here), bf),
-            pltpu.VMEM((EXTRA, rows_here), bf),
+            pltpu.VMEM((feat_here + EXTRA, rows_here), bf),
             pltpu.VMEM((1, rows_here), i32),
             pltpu.VMEM((owners // 2, capacity, rows_here), bf),
             pltpu.VMEM((16, per * capacity), bf),

time: 37.4 us -> 37.2 us (level)
  no operation moved by 1% of the time
where the time goes in v7:
time: 37.2 us; the launch traced here: 37 us
  Pallas kernels  36.3 us (98%)
  between operations  0.64 us (2%)
    pallas_call x1, Pallas kernels, on_device(): pl.pallas_call(functools.partial(exchange_kernel, owners, feat_devs, node...  30.7 us
    pallas_call x1, Pallas kernels, on_device(): pl.pallas_call(finish_kernel, grid=(feat_here // GROUP,), out_shape=tuple...  5.6 us

profile of v7, /device:TPU:0, one launch (start us, length us, event | category | flops | bytes accessed | tf_op | source)
XLA Modules:
  0.0 37.0 jit_solution(7852497092309437007)
XLA Ops:
  0.6 30.7 %exchange.1 = (bf16[2,64,512]{2,1,0:T(8,128)(2,1)}, bf16[2,16,128]{2,1,0:T(8,128)(2,1)}, f32[32,64,128]{2,1,0:T(8,128)}) custom-call(s32[64,2048]{1,0:T(8,128)} %bitcast.9, s32[1,2048]{1,0:T(1,128)} %bitcast.10, f32[1,2048]{1,0:T(1,128)} %bitcast.11, f32[1,2048]{1,0:T(1,128)} %bitcast.12, f32[1,2048]{1,0:T(1,128)} %bitcast.13, s32[1,8]{1,0:T(1,128)} %bitcast.14, ...), custom_call_target="tpu_custom_call" | custom-call | tf_op jit(solution)/shard_map/exchange/pallas_call | solution.py:396
  31.4 5.6 %finish.1 = (f32[1,3,64,256]{3,2,1,0:T(8,128)}, f32[2,3,64,256]{3,2,1,0:T(8,128)}, f32[4,3,64,256]{3,2,1,0:T(8,128)}) custom-call(bf16[2,64,512]{2,1,0:T(8,128)(2,1)} %get-tuple-element.6.late_ref, bf16[2,16,128]{2,1,0:T(8,128)(2,1)} %get-tuple-element.7.extra_ref, f32[32,64,128]{2,1,0:T(8,128)} %get-tuple-element.8.acc_ref), custom_call_target="tpu_custom_call" | custom-call | tf_op jit(solution)/shard_map/finish/pallas_call | solution.py:449
